TPU v7x, 128 devices: a whole 4x4x4 slice. The times are simulated.
128 devices in a mesh: roll: 8 (over x_lo, y), head: 16 (over x_hi, z, core).
Axes of the slice: x: 4 (x_hi: 2, x_lo: 2; x = x_hi * 2 + x_lo), y: 4, z: 4, core: 2. Of those that a mesh axis runs over, the one named last changes fastest.
Arguments:
- queries: bfloat16 [16, 1024, 8192], P('roll', None, 'head'), may hold values from -0.5 to 0.5
- keys: bfloat16 [16, 1024, 8192], P('roll', None, 'head'), may hold values from -0.5 to 0.5
- values: bfloat16 [16, 1024, 8192], P('roll', None, 'head'), may hold values from -6 to 6
- out_grad: bfloat16 [16, 1024, 8192], P('roll', None, 'head'), may hold values from -6 to 6
- prompt_keys: bfloat16 [8, 1024, 8192], P('roll', None, 'head'), may hold values from -0.5 to 0.5
- prompt_values: bfloat16 [8, 1024, 8192], P('roll', None, 'head'), may hold values from -6 to 6
- rollout_prompt: int32 [16], P('roll'), may hold values from 0 to 7
- roll_lengths: int32 [16], P('roll'), may hold values from 128 to 1024, as said below
- decay_exp: int32 [64], P('head'), may hold values from 5 to 14
- gain: bfloat16 [8192], P('head'), may hold values from 0.099609375 to 1.8984375
Outputs:
- normed: bfloat16 [16, 1024, 8192], P('roll', None, 'head')
- query_grad: bfloat16 [16, 1024, 8192], P('roll', None, 'head')
- key_grad: bfloat16 [16, 1024, 8192], P('roll', None, 'head')
- value_grad: bfloat16 [16, 1024, 8192], P('roll', None, 'head')
- prompt_key_grad: bfloat16 [8, 1024, 8192], P('roll', None, 'head')
- prompt_value_grad: bfloat16 [8, 1024, 8192], P('roll', None, 'head')
Inputs may be any that keep to these rules, and one draw needn't show every extreme that they name: `roll_lengths`: some rollout in every draw has all 1024 slots live.
All inputs are finite; a program needn't handle non-finite values.
Results may differ from a plain program's by a relative error of at most 0.0011.
Values sent between devices are 32-bit elements; how exact they have to be, the bound alone decides.
A program may use at most 192 MiB of HBM per device.

v0:
```python
import jax
import jax.numpy as jnp
from jax import lax
from jax.sharding import PartitionSpec as P

HEADS = 64
DH = 128
LEN = 1024
PLEN = 1024


HI = lax.Precision.HIGHEST
EPS = 1e-06


def spread(shard, axis, root):
    mine = lax.axis_index(axis) == root
    return lax.psum(jnp.where(mine, shard, jnp.zeros_like(shard)), axis)


def block_of():
    return 256


def decay_rates(decay_exp, total):
    return jnp.exp2(-decay_exp.astype(jnp.float32)) * (2048.0 / total)


def tables(rate, block):
    pos = jnp.arange(block).astype(jnp.float32)
    gap = pos[:, None] - pos[None, :]
    intra = jnp.where(gap >= 0.0, jnp.exp(-rate[:, None, None] * jnp.maximum(gap, 0.0)[None]), 0.0)
    qdecay = jnp.exp(-rate[None, :] * (pos[:, None] + 1.0))
    kdecay = jnp.exp(-rate[None, :] * (block - 1.0 - pos[:, None]))
    bdecay = jnp.exp(-rate * block)
    return (intra, qdecay, kdecay, bdecay)


def attend(query, key, value, start, rate):
    length, heads, width = query.shape
    block = block_of()
    count = length // block
    intra, qdecay, kdecay, bdecay = tables(rate, block)

    def attend_step(state, pieces):
        qc, kc, vc = pieces
        scores = jnp.einsum("ihd,jhd->hij", qc, kc, precision=HI) * intra
        out = jnp.einsum("hij,jhe->ihe", scores, vc, precision=HI)
        out = out + jnp.einsum("ihd,hde->ihe", qc, state, precision=HI) * qdecay[:, :, None]
        state = state * bdecay[:, None, None] + jnp.einsum(
            "jhd,jhe->hde", kc * kdecay[:, :, None], vc, precision=HI
        )
        return (state, out)

    split = lambda arr: arr.reshape(count, block, heads, width)
    final, outs = lax.scan(attend_step, start, (split(query), split(key), split(value)))
    return outs.reshape(length, heads, width)


def prompt_state(key, value, rate):
    length, heads, width = key.shape
    block = block_of()
    count = length // block
    intra, qdecay, kdecay, bdecay = tables(rate, block)

    def prompt_step(state, pieces):
        kc, vc = pieces
        return (
            state * bdecay[:, None, None]
            + jnp.einsum("jhd,jhe->hde", kc * kdecay[:, :, None], vc, precision=HI),
            None,
        )

    split = lambda arr: arr.reshape(count, block, heads, width)
    final, unused = lax.scan(
        prompt_step, jnp.zeros((heads, width, width), jnp.float32), (split(key), split(value))
    )
    return final


def local(
    queries,
    keys,
    values,
    out_grad,
    prompt_keys,
    prompt_values,
    rollout_prompt,
    roll_lengths,
    decay_exp,
    gain,
):
    rows, length, total_width = queries.shape
    owned, plength, unused_width = prompt_keys.shape
    heads = total_width // DH
    features = HEADS * DH
    rate = decay_rates(decay_exp, PLEN + LEN)
    shape_p = (owned, plength, heads, DH)
    shape_r = (rows, length, heads, DH)
    gainf = gain.astype(jnp.float32).reshape(heads, DH)

    def states_of(kp, vp):
        return jax.vmap(lambda a, b: prompt_state(a, b, rate))(kp, vp)

    prompt_fin, pull_prompt = jax.vjp(
        states_of,
        prompt_keys.astype(jnp.float32).reshape(shape_p),
        prompt_values.astype(jnp.float32).reshape(shape_p),
    )
    empty = jnp.zeros((rows, heads, DH, DH), jnp.float32)

    def select(carry, piece, first):
        numbers = first + jnp.arange(piece.shape[0])
        pick = (rollout_prompt[:, None] == numbers[None, :]).astype(jnp.float32)
        return carry + jnp.einsum("rp,phde->rhde", pick, piece, precision=HI)

    def turn(root, carry):
        piece = spread(prompt_fin, "roll", root)
        return select(carry, piece, root * owned)

    starts = lax.fori_loop(0, lax.axis_size("roll"), turn, empty)
    live = (jnp.arange(length)[None, :] < roll_lengths[:, None]).astype(jnp.float32)[
        :, :, None, None
    ]

    def forward_for(rate_part):

        def forward(a, b, c, s):
            return jax.vmap(lambda w, x, y, z: attend(w, x, y, z, rate_part))(a, b, c, s) * live

        return forward

    query_full = queries.astype(jnp.float32).reshape(shape_r)
    key_full = keys.astype(jnp.float32).reshape(shape_r)
    value_full = values.astype(jnp.float32).reshape(shape_r)
    blocks = 2
    span = heads // blocks
    pulls = []
    pieces = []
    for index in range(blocks):
        low = index * span
        high = low + span
        piece, pull_block = jax.vjp(
            forward_for(rate[low:high]),
            query_full[:, :, low:high],
            key_full[:, :, low:high],
            value_full[:, :, low:high],
            starts[:, low:high],
        )
        pieces.append(piece)
        pulls.append(pull_block)
    attn = jnp.concatenate(pieces, axis=2)
    dyg = out_grad.astype(jnp.float32).reshape(shape_r) * gainf
    local_square = jnp.sum(attn * attn, axis=(2, 3))
    local_cross = jnp.sum(dyg * attn, axis=(2, 3))
    squares = lax.psum(local_square, "head")
    scale = lax.rsqrt(squares / features + EPS)[:, :, None, None]
    normed = (attn * scale * gainf).astype(jnp.bfloat16)
    cross = lax.psum(local_cross, "head")
    attn_grad = scale * dyg - attn * scale**3 * cross[:, :, None, None] / features
    grads_q = []
    grads_k = []
    grads_v = []
    start_parts = []
    for index in range(blocks):
        low = index * span
        high = low + span
        gq, gk, gv, start_part = pulls[index](attn_grad[:, :, low:high])
        grads_q.append(gq)
        grads_k.append(gk)
        grads_v.append(gv)
        start_parts.append(start_part)
    start_grad = jnp.concatenate(start_parts, axis=1)
    numbers = jnp.arange(owned * lax.axis_size("roll"))
    pick = (rollout_prompt[:, None] == numbers[None, :]).astype(jnp.float32)
    state_grad = lax.psum_scatter(
        jnp.einsum("rp,rhde->phde", pick, start_grad, precision=HI),
        "roll",
        scatter_dimension=0,
        tiled=True,
    )
    gkp, gvp = pull_prompt(state_grad)
    cast_r = lambda arr: arr.astype(jnp.bfloat16).reshape(rows, length, total_width)
    cast_p = lambda arr: arr.astype(jnp.bfloat16).reshape(owned, plength, total_width)
    query_grad = jnp.concatenate(grads_q, axis=2)
    key_grad = jnp.concatenate(grads_k, axis=2)
    value_grad = jnp.concatenate(grads_v, axis=2)
    return (
        normed.reshape(rows, length, total_width),
        cast_r(query_grad),
        cast_r(key_grad),
        cast_r(value_grad),
        cast_p(gkp),
        cast_p(gvp),
    )


def solution(mesh):
    placed = (
        P("roll", None, "head"),
        P("roll", None, "head"),
        P("roll", None, "head"),
        P("roll", None, "head"),
        P("roll", None, "head"),
        P("roll", None, "head"),
        P("roll"),
        P("roll"),
        P("head"),
        P("head"),
    )
    return jax.shard_map(
        local,
        mesh=mesh,
        in_specs=placed,
        out_specs=(
            P("roll", None, "head"),
            P("roll", None, "head"),
            P("roll", None, "head"),
            P("roll", None, "head"),
            P("roll", None, "head"),
            P("roll", None, "head"),
        ),
        check_vma=False,
    )
```

profile of v0, /device:TPU:0, one launch (start us, length us, event | category | flops | bytes accessed | tf_op | source)
XLA Modules:
  0.0 1164.5 jit_solution(10638694155526077499)
XLA Ops:
  16.9 3.3 copy.182
  21.8 16.1 %while.133 = (s32[]{:T(128)}, f32[1,4,128,128]{3,2,1,0:T(8,128)S(1)}, f32[4,1,256,4,128]{2,4,3,1,0:T(8,128)}, f32[1,4,1,1]{1,3,2,0:T(1,128)S(1)}, f32[4,1,256,4,...) while((s32[]{:T(128)}, ...), condition=%wide.region_1.2_spmd.clone, body=%wide.region_0.1_spmd.clone.sunk | while | flops 201786368 | bytes 4733075 | solution.py:75
  38.5 629.6 %while.134 = (s32[]{:T(128)}, f32[2,4,128,128]{3,2,1,0:T(8,128)S(1)}, s32[2]{0:T(128)S(1)}, f32[1,4,128,128]{3,2,1,0:T(8,128)S(1)}, s32[]{:T(128)}, /*index=5*/u32[]{:T(128)}, u32[]{:T(128)}, s32[]{:T(128)}) while((s32[]{:T(128)}, f32[2,4,128,128]{3,2,1,0:T(8,128)S(1)}, s32[2]{0:T(128)S(1)}, f32[1,4,128,128]{3,2,1,0:T(8,128)S(1)}, ...), condition=%wide.region_4.5_spmd.clone, body=%wide.region_2.4_spmd.clone.sunk | while | flops 524299 | bytes 3408085 | solution.py:121
  39.3 79.5 %all-reduce.3.cloned.1.call-done = f32[4,128,128]{2,1,0:T(8,128)} async-done(((f32[4,128,128]{2,1,0:T(8,128)}), f32[4,128,128]{2,1,0:T(8,128)}) %all-reduce.3.cloned.1.call-update) | async-done | bytes 262160 | tf_op jit(solution)/shard_map/while/body/eval_jaxpr/psum | solution.py:18
  120.6 76.6 %all-reduce.3.cloned.1.call-done = f32[4,128,128]{2,1,0:T(8,128)} async-done(((f32[4,128,128]{2,1,0:T(8,128)}), f32[4,128,128]{2,1,0:T(8,128)}) %all-reduce.3.cloned.1.call-update) | async-done | bytes 262160 | tf_op jit(solution)/shard_map/while/body/eval_jaxpr/psum | solution.py:18
  199.1 76.5 %all-reduce.3.cloned.1.call-done = f32[4,128,128]{2,1,0:T(8,128)} async-done(((f32[4,128,128]{2,1,0:T(8,128)}), f32[4,128,128]{2,1,0:T(8,128)}) %all-reduce.3.cloned.1.call-update) | async-done | bytes 262160 | tf_op jit(solution)/shard_map/while/body/eval_jaxpr/psum | solution.py:18
  277.6 76.2 %all-reduce.3.cloned.1.call-done = f32[4,128,128]{2,1,0:T(8,128)} async-done(((f32[4,128,128]{2,1,0:T(8,128)}), f32[4,128,128]{2,1,0:T(8,128)}) %all-reduce.3.cloned.1.call-update) | async-done | bytes 262160 | tf_op jit(solution)/shard_map/while/body/eval_jaxpr/psum | solution.py:18
  355.7 76.2 %all-reduce.3.cloned.1.call-done = f32[4,128,128]{2,1,0:T(8,128)} async-done(((f32[4,128,128]{2,1,0:T(8,128)}), f32[4,128,128]{2,1,0:T(8,128)}) %all-reduce.3.cloned.1.call-update) | async-done | bytes 262160 | tf_op jit(solution)/shard_map/while/body/eval_jaxpr/psum | solution.py:18
  433.8 76.2 %all-reduce.3.cloned.1.call-done = f32[4,128,128]{2,1,0:T(8,128)} async-done(((f32[4,128,128]{2,1,0:T(8,128)}), f32[4,128,128]{2,1,0:T(8,128)}) %all-reduce.3.cloned.1.call-update) | async-done | bytes 262160 | tf_op jit(solution)/shard_map/while/body/eval_jaxpr/psum | solution.py:18
  512.0 76.6 %all-reduce.3.cloned.1.call-done = f32[4,128,128]{2,1,0:T(8,128)} async-done(((f32[4,128,128]{2,1,0:T(8,128)}), f32[4,128,128]{2,1,0:T(8,128)}) %all-reduce.3.cloned.1.call-update) | async-done | bytes 262160 | tf_op jit(solution)/shard_map/while/body/eval_jaxpr/psum | solution.py:18
  590.4 76.6 %all-reduce.3.cloned.1.call-done = f32[4,128,128]{2,1,0:T(8,128)} async-done(((f32[4,128,128]{2,1,0:T(8,128)}), f32[4,128,128]{2,1,0:T(8,128)}) %all-reduce.3.cloned.1.call-update) | async-done | bytes 262160 | tf_op jit(solution)/shard_map/while/body/eval_jaxpr/psum | solution.py:18
  687.8 3.9 copy.187
  691.7 4.0 fusion.205
  705.4 64.0 %while.136 = (s32[]{:T(128)}, f32[2,2,128,128]{3,2,1,0:T(8,128)S(1)}, f32[4,2,256,2,128]{4,2,0,3,1:T(8,128)}, f32[4,2,2,256,256]{4,3,2,1,0:T(8,128)}, f32[4,2,2,...) while((s32[]{:T(128)}, ...), condition=%wide.region_8.9_spmd.clone.clone, body=%wide.region_7.8_spmd.clone.clone.sunk | while | flops 1209140224 | bytes 13714601 | solution.py:56
  705.5 3.2 bitcast_dynamic-update-slice_fusion.10
  721.5 3.2 bitcast_dynamic-update-slice_fusion.10
  737.5 3.2 bitcast_dynamic-update-slice_fusion.10
  753.4 3.3 bitcast_dynamic-update-slice_fusion.10
  772.2 3.1 copy.190
  778.2 3.1 copy.191
  790.9 68.9 %while.135 = (s32[]{:T(128)}, f32[2,2,128,128]{3,2,1,0:T(8,128)S(1)}, f32[4,2,256,2,128]{4,2,0,3,1:T(8,128)}, f32[4,2,2,256,256]{4,3,2,1,0:T(8,128)}, f32[4,2,2,...) while((s32[]{:T(128)}, ...), condition=%wide.region_6.7_spmd.clone.clone, body=%wide.region_5.6_spmd.clone.clone.sunk | while | flops 1209140224 | bytes 13714605 | solution.py:56
  791.2 3.2 bitcast_dynamic-update-slice_fusion.8
  796.2 3.1 fusion.295
  808.4 3.2 bitcast_dynamic-update-slice_fusion.8
  825.6 3.2 bitcast_dynamic-update-slice_fusion.8
  830.5 3.1 fusion.295
  842.8 3.2 bitcast_dynamic-update-slice_fusion.8
  847.7 3.1 fusion.295
  865.7 5.4 copy.202
  871.1 3.9 copy.203
  875.0 3.5 fusion.191
  878.5 65.1 %all-reduce = (f32[2,1024]{1,0:T(2,128)S(1)}, f32[2,1024]{1,0:T(2,128)S(1)}) all-reduce(f32[2,1024]{1,0:T(2,128)S(1)} %get-tuple-element.2113, f32[2,1024]{1,0:T(2,128)S(1)} %fusion.191), channel_id=1, replica_groups=mesh['roll'=8,'head'=16] {'head'}, use_global_device_ids=true, to_apply=%region_10.11 | all-reduce | flops 4096 | bytes 32768 | tf_op jit(solution)/shard_map/psum | solution.py:156
  943.7 4.1 copy.204
  947.8 3.9 multiply_subtract_fusion
  954.1 71.8 %while.137 = (s32[]{:T(128)}, f32[2,2,128,128]{3,2,1,0:T(8,128)S(1)}, bf16[4,2,256,2,128]{4,2,0,3,1:T(8,128)(2,1)}, bf16[4,2,256,2,128]{4,2,0,3,1:T(8,128)(2,1)}...) while((s32[]{:T(128)}, ...), condition=%wide.region_14.15_spmd.clone.clone.clone, body=%wide.region_13.14_spmd.clone.clone.clone.sunk | while | flops 2417558528 | bytes 50417552 | solution.py:56
  966.7 3.1 fusion.323
  984.7 3.1 fusion.323
  1002.6 3.1 fusion.323
  1020.6 3.1 fusion.323
  1026.1 66.4 %while.138 = (s32[]{:T(128)}, f32[2,2,128,128]{3,2,1,0:T(8,128)S(1)}, bf16[4,2,256,2,128]{4,2,0,3,1:T(8,128)(2,1)}, bf16[4,2,256,2,128]{4,2,0,3,1:T(8,128)(2,1)}...) while((s32[]{:T(128)}, ...), condition=%wide.region_16.17_spmd.clone.clone.clone, body=%wide.region_15.16_spmd.clone.clone.clone.sunk | while | flops 2417558528 | bytes 50417552 | solution.py:56
  1037.7 3.1 fusion.344
  1054.2 3.1 fusion.344
  1070.7 3.1 fusion.344
  1087.2 3.1 fusion.344
  1101.2 4.2 copy.234
  1109.4 4.1 copy.233
  1125.8 9.9 reduce-scatter.2.cloned.1.call-done
  1136.6 16.2 %while.132 = (s32[]{:T(128)}, f32[1,4,128,128]{3,2,1,0:T(8,128)S(1)}, bf16[4,1,256,4,128]{4,2,3,1,0:T(8,128)(2,1)S(1)}, bf16[4,1,256,4,128]{4,2,3,1,0:T(8,128)(2...) while((s32[]{:T(128)}, ...), condition=%wide.region_19.20_spmd.clone, body=%wide.region_18.19_spmd.clone.sunk | while | flops 402850816 | bytes 3157145 | solution.py:75
  (413 shorter events, 350.1 us)
Async XLA Ops:
  9.2 4.0 copy-start.5
  16.9 3.3 copy-start.20
  21.8 16.1 %copy-start.27 = (s32[2]{0:T(128)S(1)}, s32[2]{0:T(128)}, u32[]{:S(2)}) copy-start(s32[2]{0:T(128)} %param.30) | copy-start | bytes 28
  38.5 80.2 %all-reduce.3.cloned.1.call-start = ((), (), s32[]{:S(2)}) async-start(), calls=%async_computation.2 | async-start | bytes 524288 | tf_op jit(solution)/shard_map/while/body/eval_jaxpr/psum | solution.py:18
  119.8 77.4 %all-reduce.3.cloned.1.call-start = ((), (), s32[]{:S(2)}) async-start(), calls=%async_computation.2 | async-start | bytes 524288 | tf_op jit(solution)/shard_map/while/body/eval_jaxpr/psum | solution.py:18
  198.3 77.4 %all-reduce.3.cloned.1.call-start = ((), (), s32[]{:S(2)}) async-start(), calls=%async_computation.2 | async-start | bytes 524288 | tf_op jit(solution)/shard_map/while/body/eval_jaxpr/psum | solution.py:18
  276.7 77.1 %all-reduce.3.cloned.1.call-start = ((), (), s32[]{:S(2)}) async-start(), calls=%async_computation.2 | async-start | bytes 524288 | tf_op jit(solution)/shard_map/while/body/eval_jaxpr/psum | solution.py:18
  354.9 77.1 %all-reduce.3.cloned.1.call-start = ((), (), s32[]{:S(2)}) async-start(), calls=%async_computation.2 | async-start | bytes 524288 | tf_op jit(solution)/shard_map/while/body/eval_jaxpr/psum | solution.py:18
  433.0 77.1 %all-reduce.3.cloned.1.call-start = ((), (), s32[]{:S(2)}) async-start(), calls=%async_computation.2 | async-start | bytes 524288 | tf_op jit(solution)/shard_map/while/body/eval_jaxpr/psum | solution.py:18
  511.1 77.4 %all-reduce.3.cloned.1.call-start = ((), (), s32[]{:S(2)}) async-start(), calls=%async_computation.2 | async-start | bytes 524288 | tf_op jit(solution)/shard_map/while/body/eval_jaxpr/psum | solution.py:18
  589.6 77.4 %all-reduce.3.cloned.1.call-start = ((), (), s32[]{:S(2)}) async-start(), calls=%async_computation.2 | async-start | bytes 524288 | tf_op jit(solution)/shard_map/while/body/eval_jaxpr/psum | solution.py:18
  668.1 467.6 %reduce-scatter.2.cloned.1.call-start = ((), (), s32[]{:S(2)}) async-start(), calls=%async_computation.1 | async-start | bytes 2359296 | tf_op jit(solution)/shard_map/reduce_scatter | solution.py:176
  790.9 68.9 %copy-start.26 = (s32[2]{0:T(128)S(1)}, s32[2]{0:T(128)}, u32[]{:S(2)}) copy-start(s32[2]{0:T(128)} %param.31) | copy-start | bytes 28
  862.5 3.2 copy-start.10
  865.7 5.4 copy-start.25
  954.2 4.0 copy-start.1
  958.2 4.2 copy-start.15
  962.4 4.3 copy-start.18
  964.7 5.2 copy-start.16
  972.1 4.0 copy-start.1
  976.2 4.2 copy-start.15
  980.3 4.3 copy-start.18
  982.6 5.2 copy-start.16
  990.1 4.0 copy-start.1
  994.1 4.2 copy-start.15
  998.3 4.3 copy-start.18
  1000.6 5.2 copy-start.16
  1008.0 4.0 copy-start.1
  1012.1 4.2 copy-start.15
  1016.2 4.3 copy-start.18
  1018.5 5.2 copy-start.16
  1029.2 4.2 copy-start.6
  1033.4 4.3 copy-start.12
  1035.6 5.2 copy-start.7
  1045.7 4.2 copy-start.6
  1049.9 4.3 copy-start.12
  1052.2 5.2 copy-start.7
  1062.2 4.2 copy-start.6
  1066.4 4.3 copy-start.12
  1068.7 5.2 copy-start.7
  1078.7 4.2 copy-start.6
  1082.9 4.3 copy-start.12
  1085.2 5.2 copy-start.7
  1101.2 4.3 copy-start.11
  1109.4 4.1 copy-start.8
  1109.4 4.1 copy-start.17
  1125.8 10.3 copy-start.22
  1125.8 10.3 copy-start.24
  (25 other events, 38.9 us)
Sparse Core Ops, SparseCore 0:
  42.4 76.3 all-reduce.2
  123.7 73.4 all-reduce.2
  202.2 73.4 all-reduce.2
  280.3 73.4 all-reduce.2
  358.4 73.4 all-reduce.2
  436.6 73.4 all-reduce.2
  515.0 73.4 all-reduce.2
  593.5 73.4 all-reduce.2
Sparse Core Ops, SparseCore 1:
  1096.0 39.6 reduce-scatter.1
where the time goes:
time: 1170 us; the launch traced here: 1160 us
  waiting for transfers between devices  624 us (53%)
  matrix products  225 us (19%)
  local copies, waits for them, and re-layouts  169 us (14%)
  blocking collectives  65.1 us (6%)
  other arithmetic  61.5 us (5%)
  between operations  15.9 us (1%)
    psum x8, waiting for transfers between devices, spread(): return lax.psum(jnp.where(mine, shard, jnp.zeros_like(shard)), axis)  614 us
    psum x1, blocking collectives, local(): squares = lax.psum(local_square, 'head')  65.1 us
    dot_general x24, matrix products, attend_step(): scores = jnp.einsum('ihd,jhd->hij', qc, kc, precision=HI) * intra  64.1 us
    dot_general x24, matrix products, attend_step(): out = jnp.einsum('hij,jhe->ihe', scores, vc, precision=HI)  57.6 us
    unnamed x50, local copies, waits for them, and re-layouts  47.9 us
    dot_general x24, matrix products, attend_step(): jnp.einsum('jhd,jhe->hde', kc * kdecay[:, :, None], vc, precision=HI)  44.1 us
    dynamic_update_slice x24, local copies, waits for them, and re-layouts, attend(): lax.scan(attend_step, start, (split(query), split(key), split(value)))  37.2 us
    dot_general x24, matrix products, attend_step(): jnp.einsum('ihd,hde->ihe', qc, state, precision=HI) * qdecay[:, :, None]  35.4 us
  transfers between devices with their start and end apart: 9, of which 9 were waited for; matrix products, arithmetic and copies ran while one was open for 2% of the time, Pallas kernels for 0%

commit v1 on v0

v1 whole, which is shorter than its diff:
```python
import functools

import jax
import jax.numpy as jnp
from jax import lax
from jax.experimental import pallas as pl
from jax.experimental.pallas import tpu as pltpu
from jax.sharding import PartitionSpec as P

F32 = jnp.float32
BF16 = jnp.bfloat16
EPS = 1e-06
D = 128
C = 128


def nn(a, b):
    return lax.dot_general(a, b, (((1,), (0,)), ((), ())), preferred_element_type=F32)


def nt(a, b):
    return lax.dot_general(a, b, (((1,), (1,)), ((), ())), preferred_element_type=F32)


def lanes(a, b):
    return jnp.concatenate([a, b], axis=1)


def rows(a, b):
    return jnp.concatenate([a, b], axis=0)


def split(x):
    hi = x.astype(BF16)
    return hi, (x - hi.astype(F32)).astype(BF16)


def wide(x):
    return lanes(*split(x))


def tall(x):
    return rows(*split(x))


def rate_of(exponent, shape):
    return jnp.exp2(-jnp.full(shape, exponent, jnp.int32).astype(F32))


def tables(exponent):
    rate = rate_of(exponent, (C, C))
    i = lax.broadcasted_iota(jnp.int32, (C, C), 0).astype(F32)
    j = lax.broadcasted_iota(jnp.int32, (C, C), 1).astype(F32)
    gap = i - j
    decay = jnp.exp(-rate * jnp.abs(gap))
    low = jnp.where(gap >= 0.0, decay, 0.0)
    up = jnp.where(gap <= 0.0, decay, 0.0)
    qd = jnp.exp(-rate * (i + 1.0))
    kd = jnp.exp(-rate * (C - 1.0 - i))
    return low, up, qd, kd


def power(exponent, tokens):
    return jnp.exp(-rate_of(exponent, (1, D)) * float(tokens))


def cut(n):
    return pl.ds(n * C, C)


def state_of_prompt(kp, vp, kd, exponent):
    count = kp.shape[0] // C
    total = None
    for n in range(count):
        vd = vp[cut(n), :].astype(F32) * (kd * power(exponent, C * (count - 1 - n)))
        kt = kp[cut(n), :].T
        part = nn(lanes(kt, kt), tall(vd))
        total = part if total is None else total + part
    return total


def prompt_grads(kp, vp, grad, kd, exponent, gk_ref, gv_ref):
    count = kp.shape[0] // C
    flat, high = wide(grad), tall(grad)
    for n in range(count):
        decay = kd * power(exponent, C * (count - 1 - n))
        k, v = kp[cut(n), :], vp[cut(n), :]
        gk_ref[cut(n), :] = (nt(lanes(v, v), flat) * decay).astype(BF16)
        gv_ref[cut(n), :] = (nn(lanes(k, k), high) * decay).astype(BF16)


def forward_local(q_ref, k_ref, v_ref, tab, exponent, out_ref, state_ref):
    low, up, qd, kd = tab
    step = power(exponent, C)
    state = None
    for n in range(q_ref.shape[0] // C):
        q, k, v = q_ref[cut(n), :], k_ref[cut(n), :], v_ref[cut(n), :]
        out = nn(wide(nt(q, k) * low), rows(v, v))
        kt = k.T
        part = nn(lanes(kt, kt), tall(v.astype(F32) * kd))
        if n == 0:
            state_ref[n] = jnp.zeros((D, D), F32)
            state = part
        else:
            state_ref[n] = state
            out = out + qd * nn(lanes(q, q), tall(state))
            state = state * step + part
        out_ref[cut(n), :] = out


def forward_start(q_ref, g_ref, out_ref, state_ref, start, gain, size, tab, exponent, attn_ref, full_ref, sq_ref, cr_ref, first):
    low, up, qd, kd = tab
    high = tall(start)
    for n in range(q_ref.shape[0] // C):
        q = q_ref[cut(n), :]
        token = lax.broadcasted_iota(jnp.int32, (C, D), 0) + n * C
        lift = power(exponent, C * n)
        attn = out_ref[cut(n), :] + nn(lanes(q, q), high) * (qd * lift)
        attn = jnp.where(token < size, attn, 0.0)
        attn_ref[cut(n), :] = attn
        full_ref[n] = state_ref[n] + start * lift
        dyg = g_ref[cut(n), :].astype(F32) * gain
        square, cross = attn * attn, dyg * attn
        sq_ref[cut(n), :] = jnp.where(first, 0.0, sq_ref[cut(n), :]) + square
        cr_ref[cut(n), :] = jnp.where(first, 0.0, cr_ref[cut(n), :]) + cross


def row_sums(x):
    return nt(jnp.ones((8, 2 * D), BF16), wide(x))


def column(row):
    i = lax.broadcasted_iota(jnp.int32, (C, C), 0)
    j = lax.broadcasted_iota(jnp.int32, (C, C), 1)
    spread = jnp.where(i == j, row, 0.0)
    return nn(wide(spread), jnp.ones((2 * C, D), BF16))


def start_back(q_ref, g_ref, attn_ref, s_ref, c_ref, gain, tab, exponent, normed_ref, hi_ref, lo_ref, grad_ref):
    low, up, qd, kd = tab
    step = power(exponent, C)
    total = None
    count = q_ref.shape[0] // C
    for n in reversed(range(count)):
        attn = attn_ref[cut(n), :]
        s, c = s_ref[cut(n), :], c_ref[cut(n), :]
        sg = s * gain
        normed_ref[cut(n), :] = (attn * sg).astype(BF16)
        grad = sg * g_ref[cut(n), :].astype(F32) - c * attn
        hi, lo = split(grad)
        hi_ref[cut(n), :] = hi
        lo_ref[cut(n), :] = lo
        qt = q_ref[cut(n), :].T
        part = nn(lanes(qt, qt), tall(grad * qd))
        grad_ref[n] = jnp.zeros((D, D), F32) if total is None else total
        total = part if total is None else total * step + part
    return total


def backward(q_ref, k_ref, v_ref, hi_ref, lo_ref, full_ref, grad_ref, tab, dq_ref, dk_ref, dv_ref):
    low, up, qd, kd = tab
    for n in range(q_ref.shape[0] // C):
        q, k, v = q_ref[cut(n), :], k_ref[cut(n), :], v_ref[cut(n), :]
        hi, lo = hi_ref[cut(n), :], lo_ref[cut(n), :]
        do = lanes(hi, lo)
        v2 = lanes(v, v)
        da = nt(do, v2) * low
        sh, sl = split(full_ref[n])
        ds = nt(do, rows(lanes(sh, sh), lanes(sl, sl)))
        dq = nn(wide(da), rows(k, k)) + qd * (ds[:, :D] + ds[:, D:])
        dq_ref[cut(n), :] = dq.astype(BF16)
        back = grad_ref[n]
        bh, bl = split(back)
        db = nt(v2, do) * up
        dk = nn(wide(db), rows(q, q)) + kd * nt(v2, lanes(bh, bl))
        dk_ref[cut(n), :] = dk.astype(BF16)
        pt = nt(k, q) * up
        dv2 = nn(wide(pt), rows(do, do))
        dv = dv2[:, :D] + dv2[:, D:] + kd * nn(lanes(k, k), rows(bh, bl))
        dv_ref[cut(n), :] = dv.astype(BF16)


def call(kernel, grid, ins, outs, scratch=()):
    return pl.pallas_call(
        kernel,
        grid=grid,
        in_specs=[spec for spec, _ in ins],
        out_specs=[spec for spec, _ in outs],
        out_shape=[shape for _, shape in outs],
        scratch_shapes=scratch,
        compiler_params=pltpu.CompilerParams(vmem_limit_bytes=48 * 1024 * 1024),
    )(*[arr for _, arr in ins])


SMEM = pl.BlockSpec(memory_space=pltpu.SMEM)


def local(q, k, v, g, pk, pv, which, sizes, decay, gain, features):
    rolls, length, width = q.shape
    heads = width // D
    count = length // C
    gain2 = gain.reshape(1, width)
    tok = pl.BlockSpec((1, length, D), lambda r, h: (r, 0, h))
    ptok = pl.BlockSpec((1, length, D), lambda h: (0, 0, h))
    gspec = pl.BlockSpec((1, D), lambda r, h: (0, h))
    stat = pl.BlockSpec((1, 1, count, D, D), lambda r, h: (r, h, 0, 0, 0))
    shape = jax.ShapeDtypeStruct
    states_shape = shape((rolls, heads, count, D, D), F32)

    def prompt_kernel(dec, kp, vp, out):
        e = dec[pl.program_id(0)]
        kd = tables(e)[3]
        out[0] = state_of_prompt(kp.at[0], vp.at[0], kd, e)

    (state,) = call(
        prompt_kernel, (heads,), [(SMEM, decay), (ptok, pk), (ptok, pv)],
        [(pl.BlockSpec((1, D, D), lambda h: (h, 0, 0)), shape((heads, D, D), F32))],
    )
    states = lax.all_gather(state, "roll")

    def local_kernel(dec, qr, kr, vr, out, st):
        e = dec[pl.program_id(1)]
        forward_local(qr.at[0], kr.at[0], vr.at[0], tables(e), e, out.at[0], st.at[0, 0])

    out_local, state_local = call(
        local_kernel, (rolls, heads), [(SMEM, decay), (tok, q), (tok, k), (tok, v)],
        [(tok, shape(q.shape, F32)), (stat, states_shape)],
    )

    def start_kernel(dec, wh, sz, qr, gr, gn, out, st, all_states, attn, full, msg, sq, cr):
        r, h = pl.program_id(0), pl.program_id(1)
        e = dec[h]
        start = all_states[wh[r], 0]
        forward_start(qr.at[0], gr.at[0], out.at[0], st.at[0, 0], start, gn[...].astype(F32), sz[r], tables(e), e,
                      attn.at[0], full.at[0, 0], sq, cr, h == 0)

        @pl.when(h == heads - 1)
        def _():
            msg[0, 0:1, :] = row_sums(sq[...])[0:1]
            msg[0, 1:2, :] = row_sums(cr[...])[0:1]

    attn, full, msg = call(
        start_kernel, (rolls, heads),
        [(SMEM, decay), (SMEM, which), (SMEM, sizes), (tok, q), (tok, g), (gspec, gain2), (tok, out_local), (stat, state_local),
         (pl.BlockSpec((states.shape[0], 1, D, D), lambda r, h: (0, h, 0, 0)), states)],
        [(tok, shape(q.shape, F32)), (stat, states_shape), (pl.BlockSpec((1, 2, length), lambda r, h: (r, 0, 0)), shape((rolls, 2, length), F32))],
        [pltpu.VMEM((length, D), F32), pltpu.VMEM((length, D), F32)],
    )
    sums = lax.psum(msg, "head")

    def back_kernel(dec, wh, sz, qr, gr, gn, at, sm, normed, hi, lo, gst, picked, sb, cb):
        r, h = pl.program_id(1), pl.program_id(0)
        e = dec[h]
        ss, cross = sm[0, 0:1, :], sm[0, 1:2, :]
        token = lax.broadcasted_iota(jnp.int32, (1, length), 1)
        scale = lax.rsqrt(ss / features + EPS)
        scale = jnp.where(token < sz[r], scale, 0.0)
        coef = scale * scale * scale * cross / features
        for n in range(count):
            sb[cut(n), :] = column(scale[:, n * C:(n + 1) * C])
            cb[cut(n), :] = column(coef[:, n * C:(n + 1) * C])
        total = start_back(qr.at[0], gr.at[0], at.at[0], sb, cb, gn[...].astype(F32), tables(e), e, normed.at[0], hi.at[0], lo.at[0], gst.at[0, 0])
        for p in range(states.shape[0]):
            old = jnp.where(r == 0, 0.0, picked[p, 0])
            picked[p, 0] = old + jnp.where(wh[r] == p, total, 0.0)

    tok2 = pl.BlockSpec((1, length, D), lambda h, r: (r, 0, h))
    stat2 = pl.BlockSpec((1, 1, count, D, D), lambda h, r: (r, h, 0, 0, 0))
    normed, hi, lo, back, picked = call(
        back_kernel, (heads, rolls),
        [(SMEM, decay), (SMEM, which), (SMEM, sizes), (tok2, q), (tok2, g), (pl.BlockSpec((1, D), lambda h, r: (0, h)), gain2), (tok2, attn),
         (pl.BlockSpec((1, 2, length), lambda h, r: (r, 0, 0)), sums)],
        [(tok2, shape(q.shape, BF16)), (tok2, shape(q.shape, BF16)), (tok2, shape(q.shape, BF16)), (stat2, states_shape),
         (pl.BlockSpec((states.shape[0], 1, D, D), lambda h, r: (0, h, 0, 0)), shape(states.shape, F32))],
        [pltpu.VMEM((length, D), F32), pltpu.VMEM((length, D), F32)],
    )
    owned = lax.psum_scatter(picked, "roll", scatter_dimension=0, tiled=True)

    def grads_kernel(dec, qr, kr, vr, hr, lr, fl, bk, dq, dk, dv):
        e = dec[pl.program_id(1)]
        backward(qr.at[0], kr.at[0], vr.at[0], hr.at[0], lr.at[0], fl.at[0, 0], bk.at[0, 0], tables(e), dq.at[0], dk.at[0], dv.at[0])

    dq, dk, dv = call(
        grads_kernel, (rolls, heads),
        [(SMEM, decay), (tok, q), (tok, k), (tok, v), (tok, hi), (tok, lo), (stat, full), (stat, back)],
        [(tok, shape(q.shape, BF16))] * 3,
    )

    def last_kernel(dec, kp, vp, gr, gk, gv):
        e = dec[pl.program_id(0)]
        prompt_grads(kp.at[0], vp.at[0], gr[0, 0], tables(e)[3], e, gk.at[0], gv.at[0])

    gkp, gvp = call(
        last_kernel, (heads,),
        [(SMEM, decay), (ptok, pk), (ptok, pv), (pl.BlockSpec((1, 1, D, D), lambda h: (0, h, 0, 0)), owned)],
        [(ptok, shape(pk.shape, BF16))] * 2,
    )
    return normed, dq, dk, dv, gkp, gvp


def solution(mesh):
    wide_spec = P("roll", None, "head")

    def run(q, k, v, g, pk, pv, which, sizes, decay, gain):
        body = functools.partial(local, features=gain.shape[0])
        return jax.shard_map(
            body,
            mesh=mesh,
            in_specs=(wide_spec,) * 6 + (P("roll"), P("roll"), P("head"), P("head")),
            out_specs=(wide_spec,) * 6,
            check_vma=False,
        )(q, k, v, g, pk, pv, which, sizes, decay, gain)

    return run
```

time: 1170 us -> 203 us (0.17)
  waiting for transfers between devices: 624 us -> 44.1 us
  matrix products: 225 us -> 0 us
  local copies, waits for them, and re-layouts: 169 us -> 14.5 us
  Pallas kernels: 0 us -> 64.3 us
  other arithmetic: 61.5 us -> 0 us
    psum x8 -> x0, waiting for transfers between devices: 614 us -> none  [spread(): return lax.psum(jnp.where(mine, shard, jnp.zeros_like(shard)), axis)]
    dot_general x109 -> x0, matrix products: 225 us -> none  [the longest x24 64.1 us: attend_step(): scores = jnp.einsum('ihd,jhd->hij', qc, kc, precision=HI) * intra]
    pallas_call x0 -> x6, Pallas kernels: none -> 64.3 us  [call(): pl.pallas_call(kernel, grid=grid, in_specs=[spec for spec, _ in ins], out...]
    dynamic_update_slice x24 -> x0, local copies, waits for them, and re-layouts: 37.2 us -> none  [attend(): lax.scan(attend_step, start, (split(query), split(key), split(value)))]
    unnamed x50 -> x34, local copies, waits for them, and re-layouts: 47.9 us -> 14.5 us
    all_gather x0 -> x1, waiting for transfers between devices: none -> 30.7 us  [local(): states = lax.all_gather(state, 'roll')]
    slice x10 -> x0, local copies, waits for them, and re-layouts: 25.4 us -> none  [the longest x3 9.91 us: local(): query_full[:, :, low:high]]
    dynamic_update_slice x12 -> x0, other arithmetic: 19.3 us -> none  [the longest x8 15.9 us: attend(): lax.scan(attend_step, start, (split(query), split(key), split(value)))]
  transfers between devices with their start and end apart: 9 -> 2, of which waited for: 9 -> 2; matrix products, arithmetic and copies ran while one was open for 2% -> 0% of each run, Pallas kernels for 0% -> 17%
where the time goes in v1:
time: 203 us; the launch traced here: 202 us
  blocking collectives  64.9 us (32%)
  Pallas kernels  64.3 us (32%)
  waiting for transfers between devices  44.1 us (22%)
  local copies, waits for them, and re-layouts  14.5 us (7%)
  between operations  14.1 us (7%)
    psum x1, blocking collectives, local(): sums = lax.psum(msg, 'head')  64.9 us
    pallas_call x6, Pallas kernels, call(): pl.pallas_call(kernel, grid=grid, in_specs=[spec for spec, _ in ins], out...  64.3 us
    all_gather x1, waiting for transfers between devices, local(): states = lax.all_gather(state, 'roll')  30.7 us
    unnamed x34, local copies, waits for them, and re-layouts  14.5 us
    reduce_scatter x1, waiting for transfers between devices, local(): owned = lax.psum_scatter(picked, 'roll', scatter_dimension=0, tiled=True)  13.3 us
  transfers between devices with their start and end apart: 2, of which 2 were waited for; matrix products, arithmetic and copies ran while one was open for 0% of the time, Pallas kernels for 17%

profile of v1, /device:TPU:0, one launch (start us, length us, event | category | flops | bytes accessed | tf_op | source)
XLA Modules:
  0.0 201.9 jit_solution(4966769445341067540)
XLA Ops:
  7.2 0.0 copy-start
  7.2 0.0 all-gather.3.cloned.1.call-start
  7.2 0.0 copy-start.5
  7.2 1.4 copy-done.5
  8.6 0.0 copy-start.7
  8.6 1.2 copy-done.7
  9.8 0.0 copy-start.12
  9.8 0.7 copy-done.12
  10.5 0.0 copy-start.16
  10.5 0.0 copy-start.13
  10.5 3.1 %shard_map.146 = f32[4,128,128]{2,1,0:T(8,128)} custom-call(s32[4]{0:T(128)S(1)} %copy-done.12, bf16[1,1024,512]{2,1,0:T(8,128)(2,1)S(1)} %copy-done.5, bf16[1,1024,512]{2,1,0:T(8,128)(2,1)S(1)} %copy-done.7), custom_call_target="tpu_custom_call" | custom-call | tf_op jit(solution)/shard_map/pallas_call | solution.py:184
  13.5 0.0 all-gather.3.cloned.1.call-update
  13.6 0.0 reduce-scatter.2.cloned.1.call-start
  13.6 0.0 copy-done.16
  13.6 0.0 copy-done
  13.6 0.0 copy-done.13
  13.6 0.0 copy-start.3
  13.7 1.6 copy-done.3
  15.2 0.0 copy-start.14
  15.2 0.0 copy-start.15
  15.2 11.9 %shard_map.145 = (f32[2,1024,512]{2,1,0:T(8,128)}, f32[2,4,8,128,128]{4,3,2,1,0:T(8,128)}) custom-call(s32[4]{0:T(128)S(1)} %copy-done.13, bf16[2,1024,512]{2,1,0:T(8,128)(2,1)S(1)} %copy-done, bf16[2,1024,512]{2,1,0:T(8,128)(2,1)S(1)} %copy-done.3, bf16[2,1024,512]{2,1,0:T(8,128)(2,1)} %vr.3), custom_call_target="tpu_custom_call" | custom-call | tf_op jit(solution)/shard_map/pallas_call | solution.py:184
  27.1 30.7 %all-gather.3.cloned.1.call-done = f32[32,128,128]{2,1,0:T(8,128)} async-done(((f32[4,128,128]{2,1,0:T(8,128)}), f32[32,128,128]{2,1,0:T(8,128)}) %all-gather.3.cloned.1.call-update) | async-done | bytes 2097168 | tf_op jit(solution)/shard_map/all_gather | solution.py:219
  57.8 0.0 copy-done.14
  57.8 0.0 copy-done.15
  57.8 0.0 copy-start.2
  57.8 1.6 copy-done.2
  59.4 11.4 %shard_map.147 = (f32[2,1024,512]{2,1,0:T(8,128)}, f32[2,4,8,128,128]{4,3,2,1,0:T(8,128)}, f32[2,2,1024]{2,1,0:T(2,128)S(1)}) custom-call(s32[4]{0:T(128)S(1)} %copy-done.13, s32[2]{0:T(128)S(1)} %copy-done.14, s32[2]{0:T(128)S(1)} %copy-done.15, bf16[2,1024,512]{2,1,0:T(8,128)(2,1)S(1)} %copy-done, bf16[2,1024,512]{2,1,0:T(8,128)(2,1)S(1)} %copy-done.2, ...), custom_call_target="tpu_custom_call" | custom-call | tf_op jit(solution)/shard_map/pallas_call | solution.py:184
  70.9 64.9 %psum.7.sm = f32[2,2,1024]{2,1,0:T(2,128)S(1)} all-reduce(f32[2,2,1024]{2,1,0:T(2,128)S(1)} %get-tuple-element.24), channel_id=1, replica_groups=mesh['roll'=8,'head'=16] {'head'}, use_global_device_ids=true, to_apply=%region_0.0 | all-reduce | flops 4096 | bytes 32768 | tf_op jit(solution)/shard_map/psum | solution.py:249
  135.8 11.5 %shard_map.148 = (bf16[2,1024,512]{2,1,0:T(8,128)(2,1)}, bf16[2,1024,512]{2,1,0:T(8,128)(2,1)S(1)}, bf16[2,1024,512]{2,1,0:T(8,128)(2,1)S(1)}, f32[2,4,8,128,128]{4,3,2,1,0:T(8,128)}, f32[8,4,128,128]{3,2,1,0:T(8,128)}) custom-call(s32[4]{0:T(128)S(1)} %copy-done.13, s32[2]{0:T(128)S(1)} %copy-done.14, s32[2]{0:T(128)S(1)} %copy-done.15, ...), custom_call_target="tpu_custom_call" | custom-call | tf_op jit(solution)/shard_map/pallas_call | solution.py:184
  147.3 0.0 copy-start.9
  147.3 1.3 copy-done.9
  148.7 0.0 copy-start.10
  148.7 1.4 copy-done.10
  150.0 0.0 copy-start.1
  150.0 0.0 reduce-scatter.2.cloned.1.call-update
  150.0 1.6 copy-done.1
  151.6 0.0 copy-start.4
  151.6 1.6 copy-done.4
  153.2 0.0 copy-start.6
  153.2 22.8 %shard_map.149 = (bf16[2,1024,512]{2,1,0:T(8,128)(2,1)}, bf16[2,1024,512]{2,1,0:T(8,128)(2,1)}, bf16[2,1024,512]{2,1,0:T(8,128)(2,1)}) custom-call(s32[4]{0:T(128)S(1)} %copy-done.13, bf16[2,1024,512]{2,1,0:T(8,128)(2,1)S(1)} %copy-done.1, bf16[2,1024,512]{2,1,0:T(8,128)(2,1)S(1)} %copy-done.4, bf16[2,1024,512]{2,1,0:T(8,128)(2,1)} %vr.3, ...), custom_call_target="tpu_custom_call" | custom-call | tf_op jit(solution)/shard_map/pallas_call | solution.py:184
  176.0 13.3 %reduce-scatter.2.cloned.1.call-done.gr = f32[1,4,128,128]{3,2,1,0:T(8,128)} async-done(((f32[8,4,128,128]{3,2,1,0:T(8,128)}), f32[1,4,128,128]{3,2,1,0:T(8,128)}) %reduce-scatter.2.cloned.1.call-update) | async-done | bytes 262160 | tf_op jit(solution)/shard_map/reduce_scatter | solution.py:277
  189.3 0.0 copy-done.6
  189.3 0.0 copy-start.8
  189.3 1.2 copy-done.8
  190.5 0.0 copy-start.11
  190.5 0.9 copy-done.11
  191.5 3.6 %shard_map.150 = (bf16[1,1024,512]{2,1,0:T(8,128)(2,1)}, bf16[1,1024,512]{2,1,0:T(8,128)(2,1)}) custom-call(s32[4]{0:T(128)S(1)} %copy-done.13, bf16[1,1024,512]{2,1,0:T(8,128)(2,1)S(1)} %copy-done.6, bf16[1,1024,512]{2,1,0:T(8,128)(2,1)S(1)} %copy-done.8, f32[1,4,128,128]{3,2,1,0:T(8,128)S(1)} %copy-done.11), custom_call_target="tpu_custom_call" | custom-call | tf_op jit(solution)/shard_map/pallas_call | solution.py:184
  (1 shorter events, 0.0 us)
Async XLA Ops:
  7.2 6.5 %copy-start = (bf16[2,1024,512]{2,1,0:T(8,128)(2,1)S(1)}, bf16[2,1024,512]{2,1,0:T(8,128)(2,1)}, u32[]{:S(2)}) copy-start(bf16[2,1024,512]{2,1,0:T(8,128)(2,1)} %qr.7) | copy-start | bytes 6291460
  7.2 50.7 %all-gather.3.cloned.1.call-start = ((), (), s32[]{:S(2)}) async-start(), calls=%async_computation.2 | async-start | bytes 2359296 | tf_op jit(solution)/shard_map/all_gather | solution.py:219
  7.2 1.4 copy-start.5
  8.6 1.2 copy-start.7
  9.8 0.7 copy-start.12
  10.5 3.1 %copy-start.16 = (bf16[512]{0:T(512)(128)(2,1)S(1)}, bf16[512]{0:T(512)(128)(2,1)}, u32[]{:S(2)}) copy-start(bf16[512]{0:T(512)(128)(2,1)} %param.19) | copy-start | bytes 3076
  10.5 3.2 %copy-start.13 = (s32[4]{0:T(128)S(1)}, s32[4]{0:T(128)}, u32[]{:S(2)}) copy-start(s32[4]{0:T(128)} %dec.11) | copy-start | bytes 52
  13.6 175.7 %reduce-scatter.2.cloned.1.call-start = ((), (), s32[]{:S(2)}) async-start(), calls=%async_computation.1 | async-start | bytes 2359296 | tf_op jit(solution)/shard_map/reduce_scatter | solution.py:277
  13.6 1.6 copy-start.3
  15.2 42.6 %copy-start.14 = (s32[2]{0:T(128)S(1)}, s32[2]{0:T(128)}, u32[]{:S(2)}) copy-start(s32[2]{0:T(128)} %wh.3) | copy-start | bytes 28
  15.2 42.6 %copy-start.15 = (s32[2]{0:T(128)S(1)}, s32[2]{0:T(128)}, u32[]{:S(2)}) copy-start(s32[2]{0:T(128)} %sz.3) | copy-start | bytes 28
  57.8 1.6 copy-start.2
  147.3 1.3 copy-start.9
  148.7 1.4 copy-start.10
  150.0 1.6 copy-start.1
  151.6 1.6 copy-start.4
  153.2 36.1 %copy-start.6 = (bf16[1,1024,512]{2,1,0:T(8,128)(2,1)S(1)}, bf16[1,1024,512]{2,1,0:T(8,128)(2,1)}, u32[]{:S(2)}) copy-start(bf16[1,1024,512]{2,1,0:T(8,128)(2,1)} %kp.3) | copy-start | bytes 3145732
  189.3 1.2 copy-start.8
  190.5 0.9 copy-start.11
Sparse Core Ops, SparseCore 0:
  13.7 44.1 all-gather.2
  150.2 39.0 reduce-scatter.1

commit v2 on v1

--- a/solution.py
+++ b/solution.py
@@ -180,129 +180,301 @@
         dv_ref[cut(n), :] = dv.astype(BF16)
 
 
-def call(kernel, grid, ins, outs, scratch=()):
-    return pl.pallas_call(
-        kernel,
-        grid=grid,
-        in_specs=[spec for spec, _ in ins],
-        out_specs=[spec for spec, _ in outs],
-        out_shape=[shape for _, shape in outs],
-        scratch_shapes=scratch,
-        compiler_params=pltpu.CompilerParams(vmem_limit_bytes=48 * 1024 * 1024),
-    )(*[arr for _, arr in ins])
-
-
+MESH = pl.DeviceIdType.MESH
 SMEM = pl.BlockSpec(memory_space=pltpu.SMEM)
-
-
-def local(q, k, v, g, pk, pv, which, sizes, decay, gain, features):
+ANY = pl.BlockSpec(memory_space=pl.ANY)
+ORDERS = ((0, 1, 2), (1, 2, 0), (2, 0, 1), (0, 1, 2))
+
+
+def flip(place, dim, ring):
+    if dim == 0:
+        return (place + ring) % (2 * ring)
+    if dim == 1:
+        return place + 1 - 2 * (place % 2)
+    return 2 * ring * (place // ring) + ring - 1 - place
+
+
+def choose(number, blocks, owners):
+    total = None
+    for block, owner in zip(blocks, owners):
+        part = jnp.where(number == owner, block, 0.0)
+        total = part if total is None else total + part
+    return total
+
+
+def main_kernel(
+    features, chips, ring,
+    dec, wh, sz, gain_ref, q_hbm, k_hbm, v_hbm, g_hbm, pk_hbm, pv_hbm,
+    normed_hbm, dq_hbm, dk_hbm, dv_hbm, owned_ref,
+    q_ref, k_ref, v_ref, g_ref, pk_ref, pv_ref, out_ref, st_ref, back_ref, hi_ref, lo_ref,
+    normed_ref, dq_ref, dk_ref, dv_ref, sq_ref, cr_ref, sb_ref, cb_ref, tab_ref,
+    ag_ref, agsend_ref, agrecv_ref, start_ref, sg_ref, rs1_ref, acc_ref, rs2_ref, rs3_ref,
+    tag_ref, tags_ref, msg_ref, core_ref, all_ref, sum_ref,
+    in_sem, out_sem, tag_sem, ag_sem, rs_sem, ar_sem,
+):
+    rolls, length, width = q_ref.shape
+    heads = width // D
+    count = length // C
+    me = lax.axis_index("roll")
+    head_place = lax.axis_index("head")
+    chip, core = head_place // 2, head_place % 2
+    near = [flip(me, dim, ring) for dim in range(3)]
+    sibling = chip * 2 + 1 - core
+    others = [((chip + i) % chips) * 2 + core for i in range(1, chips)]
+
+    loads = []
+    for i, (src, dst) in enumerate(((pk_hbm.at[0], pk_ref), (pv_hbm.at[0], pv_ref), (k_hbm, k_ref), (v_hbm, v_ref), (q_hbm, q_ref), (g_hbm, g_ref))):
+        copy = pltpu.make_async_copy(src, dst, in_sem.at[i])
+        copy.start()
+        loads.append(copy)
+
+    barrier = pltpu.get_barrier_semaphore()
+    for place in near:
+        pl.semaphore_signal(barrier, inc=1, device_id={"roll": place, "head": head_place}, device_id_type=MESH)
+    for place in [sibling] + others:
+        pl.semaphore_signal(barrier, inc=1, device_id={"roll": me, "head": place}, device_id_type=MESH)
+
+    def along_roll(src, dst, sems, slot, dim):
+        return pltpu.make_async_remote_copy(
+            src_ref=src, dst_ref=dst, send_sem=sems.at[0, slot], recv_sem=sems.at[1, slot],
+            device_id={"roll": near[dim], "head": head_place}, device_id_type=MESH)
+
+    def along_head(src, dst, sems, slot, place):
+        return pltpu.make_async_remote_copy(
+            src_ref=src, dst_ref=dst, send_sem=sems.at[0, slot], recv_sem=sems.at[1, slot],
+            device_id={"roll": me, "head": place}, device_id_type=MESH)
+
+    line = lax.broadcasted_iota(jnp.int32, (8, D), 0)
+    tag_ref[...] = jnp.where(line == 0, wh[0], wh[1])
+
+    def fill(h, _):
+        low, up, qd, kd = tables(dec[h])
+        tab_ref[h, 0] = low
+        tab_ref[h, 1] = up
+        tab_ref[h, 2] = qd
+        tab_ref[h, 3] = kd
+        return 0
+
+    lax.fori_loop(0, heads, fill, 0)
+
+    def tab_of(h):
+        return tab_ref[h, 0], tab_ref[h, 1], tab_ref[h, 2], tab_ref[h, 3]
+
+    def lane(h):
+        return pl.ds(pl.multiple_of(h * D, D), D)
+
+    loads[0].wait()
+    loads[1].wait()
+    pl.semaphore_wait(barrier, 3 + chips)
+
+    tag_copies = [along_roll(tag_ref, tags_ref.at[dim], tag_sem, dim, dim) for dim in range(3)]
+    for copy in tag_copies:
+        copy.start()
+
+    def gather(h, stage):
+        dim = ORDERS[h][stage]
+        src, dst = (
+            (ag_ref.at[h, pl.ds(0, 1)], ag_ref.at[h, pl.ds(1, 1)]),
+            (ag_ref.at[h, pl.ds(0, 2)], ag_ref.at[h, pl.ds(2, 2)]),
+            (agsend_ref.at[h], agrecv_ref.at[h]),
+        )[stage]
+        return along_roll(src, dst, ag_sem, 3 * h + stage, dim)
+
+    def owners_of(h):
+        first, second, third = ORDERS[h]
+        one = flip(me, first, ring)
+        return [me, one, flip(me, second, ring), flip(one, second, ring)]
+
+    gathers = [[gather(h, stage) for stage in range(3)] for h in range(heads)]
+    for h in range(heads):
+        def make_state(h):
+            ag_ref[h, 0] = state_of_prompt(pk_ref.at[:, lane(h)], pv_ref.at[:, lane(h)], tab_ref[h, 3], dec[h])
+        make_state(h)
+        gathers[h][0].start()
+
+    for copy in loads[2:5]:
+        copy.wait()
+
+    def local_unit(u, _):
+        h, r = u // rolls, u % rolls
+        view = (r, slice(None), lane(h))
+        forward_local(q_ref.at[view], k_ref.at[view], v_ref.at[view], tab_of(h), dec[h], out_ref.at[view], st_ref.at[u])
+        return 0
+
+    units = heads * rolls
+    lax.fori_loop(0, 2, local_unit, 0)
+    for h in range(heads):
+        gathers[h][0].wait()
+        gathers[h][1].start()
+    lax.fori_loop(2, 5, local_unit, 0)
+    for copy in tag_copies:
+        copy.wait()
+    for h in range(heads):
+        gathers[h][1].wait()
+        tags = tags_ref[ORDERS[h][2]]
+        for r in range(rolls):
+            agsend_ref[h, r] = choose(tags[r:r + 1, :], [ag_ref[h, k] for k in range(4)], owners_of(h))
+        gathers[h][2].start()
+    lax.fori_loop(5, units, local_unit, 0)
+    loads[5].wait()
+
+    for h in range(heads):
+        gathers[h][2].wait()
+        for r in range(rolls):
+            start_ref[h, r] = agrecv_ref[h, r] + choose(wh[r], [ag_ref[h, k] for k in range(4)], owners_of(h))
+
+        def start_unit(r, _):
+            view = (r, slice(None), pl.ds(h * D, D))
+            gain = gain_ref[:, h * D:(h + 1) * D].astype(F32)
+            forward_start(q_ref.at[view], g_ref.at[view], out_ref.at[view], st_ref.at[h * rolls + r], start_ref[h, r], gain, sz[r],
+                          tab_of(h), dec[h], out_ref.at[view], st_ref.at[h * rolls + r], sq_ref.at[r], cr_ref.at[r], h == 0)
+            return 0
+
+        lax.fori_loop(0, rolls, start_unit, 0)
+
+    def pack(total):
+        packed = None
+        for n in range(count):
+            part = jnp.where(line == n, total[:, n * C:(n + 1) * C], 0.0)
+            packed = part if packed is None else packed + part
+        return packed
+
+    for r in range(rolls):
+        msg_ref[r, 0:8] = pack(row_sums(sq_ref[r]))
+        msg_ref[r, 8:16] = pack(row_sums(cr_ref[r]))
+    swap = along_head(msg_ref.at[1 - core], core_ref.at[0], ar_sem, 0, sibling)
+    swap.start()
+    swap.wait()
+    all_ref[0] = msg_ref[core] + core_ref[0]
+    pushes = [along_head(all_ref.at[0], all_ref.at[i], ar_sem, i, others[i - 1]) for i in range(1, chips)]
+    for copy in pushes:
+        copy.start()
+    for copy in pushes:
+        copy.wait()
+    total = all_ref[0]
+    for i in range(1, chips):
+        total = total + all_ref[i]
+    sum_ref[core] = total
+    share = along_head(sum_ref.at[core], sum_ref.at[core], ar_sem, chips, sibling)
+    share.start()
+    share.wait()
+
+    for r in range(rolls):
+        ss, cross = sum_ref[r, 0:8], sum_ref[r, 8:16]
+        token = line * C + lax.broadcasted_iota(jnp.int32, (8, D), 1)
+        scale = jnp.where(token < sz[r], lax.rsqrt(ss / features + EPS), 0.0)
+        coef = scale * scale * scale * cross / features
+        for n in range(count):
+            sb_ref[r, cut(n), :] = column(scale[n:n + 1, :])
+            cb_ref[r, cut(n), :] = column(coef[n:n + 1, :])
+
+    def scatter(h, stage):
+        dim = ORDERS[h][2 - stage]
+        src, dst = (
+            (sg_ref.at[h], rs1_ref.at[h]),
+            (acc_ref.at[h, pl.ds(2, 2)], rs2_ref.at[h]),
+            (acc_ref.at[h, pl.ds(1, 1)], rs3_ref.at[h]),
+        )[stage]
+        return along_roll(src, dst, rs_sem, 3 * h + stage, dim)
+
+    scatters = [[scatter(h, stage) for stage in range(3)] for h in range(heads)]
+    for h in range(heads):
+        def back_unit(r, _):
+            view = (r, slice(None), pl.ds(h * D, D))
+            gain = gain_ref[:, h * D:(h + 1) * D].astype(F32)
+            sg_ref[h, r] = start_back(q_ref.at[view], g_ref.at[view], out_ref.at[view], sb_ref.at[r], cb_ref.at[r], gain, tab_of(h), dec[h],
+                                      normed_ref.at[view], hi_ref.at[view], lo_ref.at[view], back_ref.at[h * rolls + r])
+            return 0
+
+        lax.fori_loop(0, rolls, back_unit, 0)
+        scatters[h][0].start()
+
+    stores = [pltpu.make_async_copy(normed_ref, normed_hbm, out_sem.at[0])]
+    stores[0].start()
+
+    def back_unit2(u, _):
+        h, r = u // rolls, u % rolls
+        view = (r, slice(None), lane(h))
+        backward(q_ref.at[view], k_ref.at[view], v_ref.at[view], hi_ref.at[view], lo_ref.at[view], st_ref.at[u], back_ref.at[u], tab_of(h),
+                 dq_ref.at[view], dk_ref.at[view], dv_ref.at[view])
+        return 0
+
+    lax.fori_loop(0, 2, back_unit2, 0)
+    for h in range(heads):
+        scatters[h][0].wait()
+        tags = tags_ref[ORDERS[h][2]]
+        for k, owner in enumerate(owners_of(h)):
+            total = None
+            for r in range(rolls):
+                part = jnp.where(wh[r] == owner, sg_ref[h, r], 0.0) + jnp.where(tags[r:r + 1, :] == owner, rs1_ref[h, r], 0.0)
+                total = part if total is None else total + part
+            acc_ref[h, k] = total
+        scatters[h][1].start()
+    lax.fori_loop(2, 4, back_unit2, 0)
+    for h in range(heads):
+        scatters[h][1].wait()
+        acc_ref[h, 0] += rs2_ref[h, 0]
+        acc_ref[h, 1] += rs2_ref[h, 1]
+        scatters[h][2].start()
+    lax.fori_loop(4, units, back_unit2, 0)
+    for i, (src, dst) in enumerate(((dq_ref, dq_hbm), (dk_ref, dk_hbm), (dv_ref, dv_hbm))):
+        copy = pltpu.make_async_copy(src, dst, out_sem.at[1 + i])
+        copy.start()
+        stores.append(copy)
+    for h in range(heads):
+        scatters[h][2].wait()
+        owned_ref[h] = acc_ref[h, 0] + rs3_ref[h, 0]
+    for copy in stores:
+        copy.wait()
+
+
+def local(q, k, v, g, pk, pv, which, sizes, decay, gain, features, chips, ring):
     rolls, length, width = q.shape
     heads = width // D
     count = length // C
-    gain2 = gain.reshape(1, width)
-    tok = pl.BlockSpec((1, length, D), lambda r, h: (r, 0, h))
-    ptok = pl.BlockSpec((1, length, D), lambda h: (0, 0, h))
-    gspec = pl.BlockSpec((1, D), lambda r, h: (0, h))
-    stat = pl.BlockSpec((1, 1, count, D, D), lambda r, h: (r, h, 0, 0, 0))
+    units = heads * rolls
     shape = jax.ShapeDtypeStruct
-    states_shape = shape((rolls, heads, count, D, D), F32)
-
-    def prompt_kernel(dec, kp, vp, out):
-        e = dec[pl.program_id(0)]
-        kd = tables(e)[3]
-        out[0] = state_of_prompt(kp.at[0], vp.at[0], kd, e)
-
-    (state,) = call(
-        prompt_kernel, (heads,), [(SMEM, decay), (ptok, pk), (ptok, pv)],
-        [(pl.BlockSpec((1, D, D), lambda h: (h, 0, 0)), shape((heads, D, D), F32))],
-    )
-    states = lax.all_gather(state, "roll")
-
-    def local_kernel(dec, qr, kr, vr, out, st):
-        e = dec[pl.program_id(1)]
-        forward_local(qr.at[0], kr.at[0], vr.at[0], tables(e), e, out.at[0], st.at[0, 0])
-
-    out_local, state_local = call(
-        local_kernel, (rolls, heads), [(SMEM, decay), (tok, q), (tok, k), (tok, v)],
-        [(tok, shape(q.shape, F32)), (stat, states_shape)],
-    )
-
-    def start_kernel(dec, wh, sz, qr, gr, gn, out, st, all_states, attn, full, msg, sq, cr):
-        r, h = pl.program_id(0), pl.program_id(1)
-        e = dec[h]
-        start = all_states[wh[r], 0]
-        forward_start(qr.at[0], gr.at[0], out.at[0], st.at[0, 0], start, gn[...].astype(F32), sz[r], tables(e), e,
-                      attn.at[0], full.at[0, 0], sq, cr, h == 0)
-
-        @pl.when(h == heads - 1)
-        def _():
-            msg[0, 0:1, :] = row_sums(sq[...])[0:1]
-            msg[0, 1:2, :] = row_sums(cr[...])[0:1]
-
-    attn, full, msg = call(
-        start_kernel, (rolls, heads),
-        [(SMEM, decay), (SMEM, which), (SMEM, sizes), (tok, q), (tok, g), (gspec, gain2), (tok, out_local), (stat, state_local),
-         (pl.BlockSpec((states.shape[0], 1, D, D), lambda r, h: (0, h, 0, 0)), states)],
-        [(tok, shape(q.shape, F32)), (stat, states_shape), (pl.BlockSpec((1, 2, length), lambda r, h: (r, 0, 0)), shape((rolls, 2, length), F32))],
-        [pltpu.VMEM((length, D), F32), pltpu.VMEM((length, D), F32)],
-    )
-    sums = lax.psum(msg, "head")
-
-    def back_kernel(dec, wh, sz, qr, gr, gn, at, sm, normed, hi, lo, gst, picked, sb, cb):
-        r, h = pl.program_id(1), pl.program_id(0)
-        e = dec[h]
-        ss, cross = sm[0, 0:1, :], sm[0, 1:2, :]
-        token = lax.broadcasted_iota(jnp.int32, (1, length), 1)
-        scale = lax.rsqrt(ss / features + EPS)
-        scale = jnp.where(token < sz[r], scale, 0.0)
-        coef = scale * scale * scale * cross / features
-        for n in range(count):
-            sb[cut(n), :] = column(scale[:, n * C:(n + 1) * C])
-            cb[cut(n), :] = column(coef[:, n * C:(n + 1) * C])
-        total = start_back(qr.at[0], gr.at[0], at.at[0], sb, cb, gn[...].astype(F32), tables(e), e, normed.at[0], hi.at[0], lo.at[0], gst.at[0, 0])
-        for p in range(states.shape[0]):
-            old = jnp.where(r == 0, 0.0, picked[p, 0])
-            picked[p, 0] = old + jnp.where(wh[r] == p, total, 0.0)
-
-    tok2 = pl.BlockSpec((1, length, D), lambda h, r: (r, 0, h))
-    stat2 = pl.BlockSpec((1, 1, count, D, D), lambda h, r: (r, h, 0, 0, 0))
-    normed, hi, lo, back, picked = call(
-        back_kernel, (heads, rolls),
-        [(SMEM, decay), (SMEM, which), (SMEM, sizes), (tok2, q), (tok2, g), (pl.BlockSpec((1, D), lambda h, r: (0, h)), gain2), (tok2, attn),
-         (pl.BlockSpec((1, 2, length), lambda h, r: (r, 0, 0)), sums)],
-        [(tok2, shape(q.shape, BF16)), (tok2, shape(q.shape, BF16)), (tok2, shape(q.shape, BF16)), (stat2, states_shape),
-         (pl.BlockSpec((states.shape[0], 1, D, D), lambda h, r: (0, h, 0, 0)), shape(states.shape, F32))],
-        [pltpu.VMEM((length, D), F32), pltpu.VMEM((length, D), F32)],
-    )
-    owned = lax.psum_scatter(picked, "roll", scatter_dimension=0, tiled=True)
-
-    def grads_kernel(dec, qr, kr, vr, hr, lr, fl, bk, dq, dk, dv):
-        e = dec[pl.program_id(1)]
-        backward(qr.at[0], kr.at[0], vr.at[0], hr.at[0], lr.at[0], fl.at[0, 0], bk.at[0, 0], tables(e), dq.at[0], dk.at[0], dv.at[0])
-
-    dq, dk, dv = call(
-        grads_kernel, (rolls, heads),
-        [(SMEM, decay), (tok, q), (tok, k), (tok, v), (tok, hi), (tok, lo), (stat, full), (stat, back)],
-        [(tok, shape(q.shape, BF16))] * 3,
-    )
+    tokens = pltpu.VMEM(q.shape, BF16)
+    block = lambda *lead: pltpu.VMEM((*lead, D, D), F32)
+    dma = lambda *dims: pltpu.SemaphoreType.DMA(dims)
+    normed, dq, dk, dv, owned = pl.pallas_call(
+        functools.partial(main_kernel, features, chips, ring),
+        in_specs=[SMEM, SMEM, SMEM, pl.BlockSpec(memory_space=pltpu.VMEM)] + [ANY] * 6,
+        out_specs=[ANY] * 4 + [pl.BlockSpec(memory_space=pltpu.VMEM)],
+        out_shape=[shape(q.shape, BF16)] * 4 + [shape((heads, D, D), F32)],
+        scratch_shapes=[tokens] * 4 + [pltpu.VMEM((length, width), BF16)] * 2 + [pltpu.VMEM(q.shape, F32)]
+        + [block(units, count)] * 2 + [tokens] * 6 + [pltpu.VMEM((rolls, length, D), F32)] * 4 + [block(heads, 4)]
+        + [block(heads, 4), block(heads, 2), block(heads, 2), block(heads, 2)]
+        + [block(heads, 2), block(heads, 2), block(heads, 4), block(heads, 2), block(heads, 1)]
+        + [pltpu.VMEM((8, D), jnp.int32), pltpu.VMEM((3, 8, D), jnp.int32)]
+        + [pltpu.VMEM((rolls, 16, D), F32), pltpu.VMEM((1, 16, D), F32), pltpu.VMEM((chips, 16, D), F32), pltpu.VMEM((rolls, 16, D), F32)]
+        + [dma(6), dma(4), dma(2, 3), dma(2, 3 * heads), dma(2, 3 * heads), dma(2, chips + 1)],
+        compiler_params=pltpu.CompilerParams(vmem_limit_bytes=60 * 1024 * 1024, collective_id=0, has_side_effects=True),
+    )(decay, which, sizes, gain.reshape(1, width), q, k, v, g, pk, pv)
 
     def last_kernel(dec, kp, vp, gr, gk, gv):
         e = dec[pl.program_id(0)]
-        prompt_grads(kp.at[0], vp.at[0], gr[0, 0], tables(e)[3], e, gk.at[0], gv.at[0])
-
-    gkp, gvp = call(
-        last_kernel, (heads,),
-        [(SMEM, decay), (ptok, pk), (ptok, pv), (pl.BlockSpec((1, 1, D, D), lambda h: (0, h, 0, 0)), owned)],
-        [(ptok, shape(pk.shape, BF16))] * 2,
-    )
+        prompt_grads(kp.at[0], vp.at[0], gr[0], tables(e)[3], e, gk.at[0], gv.at[0])
+
+    ptok = pl.BlockSpec((1, length, D), lambda h: (0, 0, h))
+    gkp, gvp = pl.pallas_call(
+        last_kernel,
+        grid=(heads,),
+        in_specs=[SMEM, ptok, ptok, pl.BlockSpec((1, D, D), lambda h: (h, 0, 0))],
+        out_specs=[ptok] * 2,
+        out_shape=[shape(pk.shape, BF16)] * 2,
+        compiler_params=pltpu.CompilerParams(vmem_limit_bytes=32 * 1024 * 1024),
+    )(decay, pk, pv, owned)
     return normed, dq, dk, dv, gkp, gvp
 
 
 def solution(mesh):
     wide_spec = P("roll", None, "head")
+    chips = mesh.shape["head"] // 2
+    ring = mesh.shape["roll"] // 2
 
     def run(q, k, v, g, pk, pv, which, sizes, decay, gain):
-        body = functools.partial(local, features=gain.shape[0])
+        body = functools.partial(local, features=gain.shape[0], chips=chips, ring=ring)
         return jax.shard_map(
             body,
             mesh=mesh,

time: 203 us -> 79.9 us (0.39)
  blocking collectives: 64.9 us -> 0 us
  waiting for transfers between devices: 44.1 us -> 0 us
  between operations: 14.1 us -> 0.68 us
  local copies, waits for them, and re-layouts: 14.5 us -> 10.6 us
  Pallas kernels: 64.3 us -> 67.5 us
    psum x1 -> x0, blocking collectives: 64.9 us -> none  [local(): sums = lax.psum(msg, 'head')]
    all_gather x1 -> x0, waiting for transfers between devices: 30.7 us -> none  [local(): states = lax.all_gather(state, 'roll')]
    reduce_scatter x1 -> x0, waiting for transfers between devices: 13.3 us -> none  [local(): owned = lax.psum_scatter(picked, 'roll', scatter_dimension=0, tiled=True)]
    unnamed x34 -> x20, local copies, waits for them, and re-layouts: 14.5 us -> 9.32 us
    pallas_call x6 -> x2, Pallas kernels: 64.3 us -> 67.5 us  [the longest x1 63.9 us: local(): pl.pallas_call(functools.partial(main_kernel, features, chips, ring), in_...]
  transfers between devices with their start and end apart: 2 -> 0, of which waited for: 2 -> 0; matrix products, arithmetic and copies ran while one was open for 0% -> 0% of each run, Pallas kernels for 17% -> 0%
where the time goes in v2:
time: 79.9 us; the launch traced here: 78.8 us
  Pallas kernels  67.5 us (84%)
  local copies, waits for them, and re-layouts  10.6 us (13%)
    pallas_call x1, Pallas kernels, local(): pl.pallas_call(functools.partial(main_kernel, features, chips, ring), in_...  63.9 us
    unnamed x20, local copies, waits for them, and re-layouts  9.32 us
    pallas_call x1, Pallas kernels, local(): pl.pallas_call(last_kernel, grid=(heads,), in_specs=[SMEM, ptok, ptok, pl...  3.63 us

profile of v2, /device:TPU:0, one launch (start us, length us, event | category | flops | bytes accessed | tf_op | source)
XLA Modules:
  0.0 78.8 jit_solution(7289282569379163695)
XLA Ops:
  0.6 1.3 %reshape.15.gain_ref = bf16[1,512]{1,0:T(2,128)(2,1)} reshape(bf16[512]{0:T(512)(128)(2,1)} %param.19) | data formatting | bytes 2048 | tf_op jit(solution)/shard_map/reshape | solution.py:453
  1.9 0.0 copy-start
  1.9 0.0 copy-start.1
  1.9 0.0 copy-start.3
  1.9 63.9 %shard_map.145 = (bf16[2,1024,512]{2,1,0:T(8,128)(2,1)}, bf16[2,1024,512]{2,1,0:T(8,128)(2,1)}, bf16[2,1024,512]{2,1,0:T(8,128)(2,1)}, bf16[2,1024,512]{2,1,0:T(8,128)(2,1)}, f32[4,128,128]{2,1,0:T(8,128)}) custom-call(s32[4]{0:T(128)} %dec.3, s32[2]{0:T(128)} %wh.1, s32[2]{0:T(128)} %sz.1, bf16[1,512]{1,0:T(2,128)(2,1)} %reshape.15.gain_ref, ...), custom_call_target="tpu_custom_call" | custom-call | tf_op jit(solution)/shard_map/pallas_call | solution.py:440
  65.8 0.0 copy-done
  65.8 0.0 copy-done.1
  65.8 0.0 copy-done.3
  65.8 0.0 copy-start.2
  65.9 0.9 %copy-done.2 = f32[4,128,128]{2,1,0:T(8,128)S(1)} copy-done((f32[4,128,128]{2,1,0:T(8,128)S(1)}, f32[4,128,128]{2,1,0:T(8,128)}, u32[]{:S(2)}) %copy-start.2) | copy-done | bytes 262168
  66.8 0.0 copy-start.7
  66.8 3.6 %shard_map.146 = (bf16[1,1024,512]{2,1,0:T(8,128)(2,1)}, bf16[1,1024,512]{2,1,0:T(8,128)(2,1)}) custom-call(s32[4]{0:T(128)S(1)} %copy-done.3, bf16[1,1024,512]{2,1,0:T(8,128)(2,1)S(1)} %copy-done, bf16[1,1024,512]{2,1,0:T(8,128)(2,1)S(1)} %copy-done.1, f32[4,128,128]{2,1,0:T(8,128)S(1)} %copy-done.2), custom_call_target="tpu_custom_call" | custom-call | tf_op jit(solution)/shard_map/pallas_call | solution.py:460
  70.4 0.0 copy-done.7
  70.4 0.0 copy-start.6
  70.4 1.3 %copy.20 = bf16[2,1024,512]{2,1,0:T(8,128)(2,1)} copy(bf16[2,1024,512]{2,1,0:T(8,128)(2,1)S(1)} %copy-done.7) | data formatting | bytes 4194304
  71.8 1.0 %copy-done.6 = bf16[2,1024,512]{2,1,0:T(8,128)(2,1)S(1)} copy-done((bf16[2,1024,512]{2,1,0:T(8,128)(2,1)S(1)}, bf16[2,1024,512]{2,1,0:T(8,128)(2,1)}, u32[]{:S(2)}) %copy-start.6) | copy-done | bytes 2097176
  72.8 0.0 copy-start.5
  72.8 1.3 %copy.21 = bf16[2,1024,512]{2,1,0:T(8,128)(2,1)} copy(bf16[2,1024,512]{2,1,0:T(8,128)(2,1)S(1)} %copy-done.6) | data formatting | bytes 4194304
  74.1 1.0 %copy-done.5 = bf16[2,1024,512]{2,1,0:T(8,128)(2,1)S(1)} copy-done((bf16[2,1024,512]{2,1,0:T(8,128)(2,1)S(1)}, bf16[2,1024,512]{2,1,0:T(8,128)(2,1)}, u32[]{:S(2)}) %copy-start.5) | copy-done | bytes 2097176
  75.1 0.0 copy-start.4
  75.1 1.3 %copy.22 = bf16[2,1024,512]{2,1,0:T(8,128)(2,1)} copy(bf16[2,1024,512]{2,1,0:T(8,128)(2,1)S(1)} %copy-done.5) | data formatting | bytes 4194304
  76.4 1.0 %copy-done.4 = bf16[2,1024,512]{2,1,0:T(8,128)(2,1)S(1)} copy-done((bf16[2,1024,512]{2,1,0:T(8,128)(2,1)S(1)}, bf16[2,1024,512]{2,1,0:T(8,128)(2,1)}, u32[]{:S(2)}) %copy-start.4) | copy-done | bytes 2097176
  77.5 1.3 %copy.23 = bf16[2,1024,512]{2,1,0:T(8,128)(2,1)} copy(bf16[2,1024,512]{2,1,0:T(8,128)(2,1)S(1)} %copy-done.4) | data formatting | bytes 4194304
Async XLA Ops:
  1.9 63.9 %copy-start = (bf16[1,1024,512]{2,1,0:T(8,128)(2,1)S(1)}, bf16[1,1024,512]{2,1,0:T(8,128)(2,1)}, u32[]{:S(2)}) copy-start(bf16[1,1024,512]{2,1,0:T(8,128)(2,1)} %kp.1) | copy-start | bytes 3145732
  1.9 63.9 %copy-start.1 = (bf16[1,1024,512]{2,1,0:T(8,128)(2,1)S(1)}, bf16[1,1024,512]{2,1,0:T(8,128)(2,1)}, u32[]{:S(2)}) copy-start(bf16[1,1024,512]{2,1,0:T(8,128)(2,1)} %vp.1) | copy-start | bytes 3145732
  1.9 63.9 %copy-start.3 = (s32[4]{0:T(128)S(1)}, s32[4]{0:T(128)}, u32[]{:S(2)}) copy-start(s32[4]{0:T(128)} %dec.3) | copy-start | bytes 52
  65.8 1.0 %copy-start.2 = (f32[4,128,128]{2,1,0:T(8,128)S(1)}, f32[4,128,128]{2,1,0:T(8,128)}, u32[]{:S(2)}) copy-start(f32[4,128,128]{2,1,0:T(8,128)} %get-tuple-element.17.gr) | copy-start | bytes 786436
  66.8 3.6 %copy-start.7 = (bf16[2,1024,512]{2,1,0:T(8,128)(2,1)S(1)}, bf16[2,1024,512]{2,1,0:T(8,128)(2,1)}, u32[]{:S(2)}) copy-start(bf16[2,1024,512]{2,1,0:T(8,128)(2,1)} %get-tuple-element.26) | copy-start | bytes 6291460
  70.4 2.3 %copy-start.6 = (bf16[2,1024,512]{2,1,0:T(8,128)(2,1)S(1)}, bf16[2,1024,512]{2,1,0:T(8,128)(2,1)}, u32[]{:S(2)}) copy-start(bf16[2,1024,512]{2,1,0:T(8,128)(2,1)} %get-tuple-element.27) | copy-start | bytes 6291460
  72.8 2.3 %copy-start.5 = (bf16[2,1024,512]{2,1,0:T(8,128)(2,1)S(1)}, bf16[2,1024,512]{2,1,0:T(8,128)(2,1)}, u32[]{:S(2)}) copy-start(bf16[2,1024,512]{2,1,0:T(8,128)(2,1)} %get-tuple-element.28) | copy-start | bytes 6291460
  75.1 2.3 %copy-start.4 = (bf16[2,1024,512]{2,1,0:T(8,128)(2,1)S(1)}, bf16[2,1024,512]{2,1,0:T(8,128)(2,1)}, u32[]{:S(2)}) copy-start(bf16[2,1024,512]{2,1,0:T(8,128)(2,1)} %get-tuple-element.29) | copy-start | bytes 6291460

commit v3 on v2

v3 whole, which is shorter than its diff:
```python
import functools

import jax
import jax.numpy as jnp
from jax import lax
from jax.experimental import pallas as pl
from jax.experimental.pallas import tpu as pltpu
from jax.sharding import PartitionSpec as P

F32 = jnp.float32
BF16 = jnp.bfloat16
EPS = 1e-06
D = 128
C = 128


def nn(a, b):
    return lax.dot_general(a, b, (((1,), (0,)), ((), ())), preferred_element_type=F32)


def nt(a, b):
    return lax.dot_general(a, b, (((1,), (1,)), ((), ())), preferred_element_type=F32)


def lanes(a, b):
    return jnp.concatenate([a, b], axis=1)


def rows(a, b):
    return jnp.concatenate([a, b], axis=0)


def split(x):
    hi = x.astype(BF16)
    return hi, (x - hi.astype(F32)).astype(BF16)


def wide(x):
    return lanes(*split(x))


def tall(x):
    return rows(*split(x))


def rate_of(exponent, shape):
    return jnp.exp2(-jnp.full(shape, exponent, jnp.int32).astype(F32))


def tables(exponent):
    rate = rate_of(exponent, (C, C))
    i = lax.broadcasted_iota(jnp.int32, (C, C), 0).astype(F32)
    j = lax.broadcasted_iota(jnp.int32, (C, C), 1).astype(F32)
    gap = i - j
    decay = jnp.exp(-rate * jnp.abs(gap))
    low = jnp.where(gap >= 0.0, decay, 0.0)
    up = jnp.where(gap <= 0.0, decay, 0.0)
    qd = jnp.exp(-rate * (i + 1.0))
    kd = jnp.exp(-rate * (C - 1.0 - i))
    return low, up, qd, kd


def power(exponent, tokens):
    return jnp.exp(-rate_of(exponent, (1, D)) * float(tokens))


def cut(n):
    return pl.ds(n * C, C)


def state_of_prompt(kp, vp, kd, exponent):
    count = kp.shape[0] // C
    total = None
    for n in range(count):
        vd = vp[cut(n), :].astype(F32) * (kd * power(exponent, C * (count - 1 - n)))
        kt = kp[cut(n), :].T
        part = nn(lanes(kt, kt), tall(vd))
        total = part if total is None else total + part
    return total


def prompt_grads(kp, vp, grad, kd, exponent, gk_ref, gv_ref):
    count = kp.shape[0] // C
    flat, high = wide(grad), tall(grad)
    for n in range(count):
        decay = kd * power(exponent, C * (count - 1 - n))
        k, v = kp[cut(n), :], vp[cut(n), :]
        gk_ref[cut(n), :] = (nt(lanes(v, v), flat) * decay).astype(BF16)
        gv_ref[cut(n), :] = (nn(lanes(k, k), high) * decay).astype(BF16)


def forward_local(q_ref, k_ref, v_ref, tab, exponent, out_ref, state_ref):
    low, up, qd, kd = tab
    step = power(exponent, C)
    zero = jnp.zeros((D, C), BF16)
    count = q_ref.shape[0] // C
    state_ref[0] = jnp.zeros((D, D), F32)
    state = None
    for n in range(count - 1):
        kt = k_ref[cut(n), :].T
        part = nn(lanes(kt, kt), tall(v_ref[cut(n), :].astype(F32) * kd))
        state = part if n == 0 else state * step + part
        state_ref[n + 1] = state
    for n in range(count):
        q, k, v = q_ref[cut(n), :], k_ref[cut(n), :], v_ref[cut(n), :]
        kt = k.T
        if n == 0:
            out = nn(wide(nn(q, kt) * low), rows(v, v))
        else:
            both = nn(lanes(q, q), lanes(rows(kt, zero), tall(state_ref[n])))
            out = nn(wide(both[:, :C] * low), rows(v, v)) + qd * both[:, C:]
        out_ref[cut(n), :] = out


def forward_start(q_ref, g_ref, attn_ref, start, gain, size, tab, exponent, sq_ref, cr_ref, first):
    low, up, qd, kd = tab
    high = tall(start)
    for n in range(q_ref.shape[0] // C):
        q = q_ref[cut(n), :]
        token = lax.broadcasted_iota(jnp.int32, (C, D), 0) + n * C
        attn = attn_ref[cut(n), :] + nn(lanes(q, q), high) * (qd * power(exponent, C * n))
        attn = jnp.where(token < size, attn, 0.0)
        attn_ref[cut(n), :] = attn
        dyg = g_ref[cut(n), :].astype(F32) * gain
        square, cross = attn * attn, dyg * attn
        sq_ref[cut(n), :] = jnp.where(first, 0.0, sq_ref[cut(n), :]) + square
        cr_ref[cut(n), :] = jnp.where(first, 0.0, cr_ref[cut(n), :]) + cross


def ready(q_ref, state_ref, qs_ref, start, tab, exponent):
    low, up, qd, kd = tab
    for n in range(q_ref.shape[0] // C):
        state_ref[n] = state_ref[n] + start * power(exponent, C * n)
        hi, lo = split(q_ref[cut(n), :].astype(F32) * qd)
        qs_ref[n] = lanes(hi.T, lo.T)


def row_sums(x):
    return nt(jnp.ones((8, 2 * D), BF16), wide(x))


def column(row):
    i = lax.broadcasted_iota(jnp.int32, (C, C), 0)
    j = lax.broadcasted_iota(jnp.int32, (C, C), 1)
    spread = jnp.where(i == j, row, 0.0)
    return nn(wide(spread), jnp.ones((2 * C, D), BF16))


def start_back(qs_ref, g_ref, attn_ref, s_ref, c_ref, gain, exponent, hi_ref, lo_ref, grad_ref):
    step = power(exponent, C)
    total = None
    count = qs_ref.shape[0]
    for n in reversed(range(count)):
        attn = attn_ref[cut(n), :]
        s, c = s_ref[cut(n), :], c_ref[cut(n), :]
        hi, lo = split(s * gain * g_ref[cut(n), :].astype(F32) - c * attn)
        hi_ref[cut(n), :] = hi
        lo_ref[cut(n), :] = lo
        do = lanes(hi, lo)
        both = nn(qs_ref[n], rows(do, do))
        part = both[:, :D] + both[:, D:]
        grad_ref[n] = jnp.zeros((D, D), F32) if total is None else total
        total = part if total is None else total * step + part
    return total


def backward(q_ref, k_ref, v_ref, hi_ref, lo_ref, full_ref, grad_ref, tab, dq_ref, dk_ref, dv_ref):
    low, up, qd, kd = tab
    zero = jnp.zeros((D, C), BF16)
    for n in range(q_ref.shape[0] // C):
        q, k, v = q_ref[cut(n), :], k_ref[cut(n), :], v_ref[cut(n), :]
        hi, lo = hi_ref[cut(n), :], lo_ref[cut(n), :]
        do = lanes(hi, lo)
        vt = v.T
        sh, sl = split(full_ref[n])
        flat = lanes(vt, sh.T)
        both = nn(do, rows(flat, flat))
        ds = both[:, D:] + nn(hi, sl.T)
        dq = nn(wide(both[:, :D] * low), rows(k, k)) + qd * ds
        dq_ref[cut(n), :] = dq.astype(BF16)
        bh, bl = split(grad_ref[n])
        vb = nn(lanes(v, v), rows(lanes(hi.T, bh.T), lanes(lo.T, bl.T)))
        dk = nn(wide(vb[:, :C] * up), rows(q, q)) + kd * vb[:, C:]
        dk_ref[cut(n), :] = dk.astype(BF16)
        kb = nn(lanes(k, k), lanes(rows(q.T, zero), rows(bh, bl)))
        dv2 = nn(wide(kb[:, :C] * up), rows(do, do))
        dv = dv2[:, :D] + dv2[:, D:] + kd * kb[:, C:]
        dv_ref[cut(n), :] = dv.astype(BF16)


MESH = pl.DeviceIdType.MESH
SMEM = pl.BlockSpec(memory_space=pltpu.SMEM)
ANY = pl.BlockSpec(memory_space=pl.ANY)
TURNS = ((0, 1, 2), (1, 2, 0), (2, 0, 1))
PARTS = tuple((h, TURNS[h], 0, D) for h in range(3)) + ((3, TURNS[0], 0, 48), (3, TURNS[1], 48, 40), (3, TURNS[2], 88, 40))

def flip(place, dim, ring):
    if dim == 0:
        return (place + ring) % (2 * ring)
    if dim == 1:
        return place + 1 - 2 * (place % 2)
    return 2 * ring * (place // ring) + ring - 1 - place


def choose(number, blocks, owners):
    total = None
    for block, owner in zip(blocks, owners):
        part = jnp.where(number == owner, block, 0.0)
        total = part if total is None else total + part
    return total


def main_kernel(
    features, chips, ring,
    dec, wh, sz, gain_ref, q_hbm, k_hbm, v_hbm, g_hbm, pk_hbm, pv_hbm,
    normed_ref, dq_ref, dk_ref, dv_ref, owned_ref, pk_ref, pv_ref,
    q_ref, k_ref, v_ref, g_ref, out_ref, st_ref, back_ref, hi_ref, lo_ref, sq_ref, cr_ref, sb_ref, cb_ref, tab_ref,
    ag_ref, agsend_ref, agrecv_ref, start_ref, sg_ref, rs1_ref, acc_ref, rs2_ref, rs3_ref,
    qs_ref, gains_ref, tag_ref, tags_ref, msg_ref, all_ref,
    in_sem, tag_sem, ag_sem, rs_sem, ar_sem,
):
    rolls, length, width = q_ref.shape
    heads = width // D
    count = length // C
    me = lax.axis_index("roll")
    head_place = lax.axis_index("head")
    chip, core = head_place // 2, head_place % 2
    near = [flip(me, dim, ring) for dim in range(3)]
    others = [((chip + i) % chips) * 2 + side for i in range(chips) for side in (core, 1 - core)][1:]

    loads = []
    for i, (src, dst) in enumerate(((pk_hbm.at[0], pk_ref), (pv_hbm.at[0], pv_ref), (k_hbm, k_ref), (v_hbm, v_ref), (q_hbm, q_ref), (g_hbm, g_ref))):
        copy = pltpu.make_async_copy(src, dst, in_sem.at[i])
        copy.start()
        loads.append(copy)

    barrier = pltpu.get_barrier_semaphore()
    for place in near:
        pl.semaphore_signal(barrier, inc=1, device_id={"roll": place, "head": head_place}, device_id_type=MESH)
    for place in others:
        pl.semaphore_signal(barrier, inc=1, device_id={"roll": me, "head": place}, device_id_type=MESH)

    def along_roll(src, dst, sems, slot, dim):
        return pltpu.make_async_remote_copy(
            src_ref=src, dst_ref=dst, send_sem=sems.at[0, slot], recv_sem=sems.at[1, slot],
            device_id={"roll": near[dim], "head": head_place}, device_id_type=MESH)

    def along_head(src, dst, sems, slot, place):
        return pltpu.make_async_remote_copy(
            src_ref=src, dst_ref=dst, send_sem=sems.at[0, slot], recv_sem=sems.at[1, slot],
            device_id={"roll": me, "head": place}, device_id_type=MESH)

    line = lax.broadcasted_iota(jnp.int32, (8, D), 0)
    tag_ref[...] = jnp.where(line == 0, wh[0], wh[1])

    for h in range(heads):
        gains_ref[h] = gain_ref[pl.ds(h * D, D)].astype(F32).reshape(1, D)

    def fill(h, _):
        low, up, qd, kd = tables(dec[h])
        tab_ref[h, 0] = low
        tab_ref[h, 1] = up
        tab_ref[h, 2] = qd
        tab_ref[h, 3] = kd
        return 0

    lax.fori_loop(0, heads, fill, 0)

    def tab_of(h):
        return tab_ref[h, 0], tab_ref[h, 1], tab_ref[h, 2], tab_ref[h, 3]

    def lane(h):
        return pl.ds(pl.multiple_of(h * D, D), D)

    loads[0].wait()
    loads[1].wait()
    for h in range(heads):
        ag_ref[h, 0] = state_of_prompt(pk_ref.at[:, lane(h)], pv_ref.at[:, lane(h)], tab_ref[h, 3], dec[h])
    pl.semaphore_wait(barrier, 3 + len(others))

    tag_copies = [along_roll(tag_ref, tags_ref.at[dim], tag_sem, dim, dim) for dim in range(3)]
    for copy in tag_copies:
        copy.start()

    def owners_of(order):
        first, second, third = order
        one = flip(me, first, ring)
        return [me, one, flip(me, second, ring), flip(one, second, ring)]

    def gather(i, stage, r=0):
        h, order, low, size = PARTS[i]
        cells = pl.ds(low, size)
        src, dst, dim = (
            (ag_ref.at[h, 0, cells], ag_ref.at[h, 1, cells], order[0]),
            (ag_ref.at[h, 0, cells], ag_ref.at[h, 2, cells], order[1]),
            (ag_ref.at[h, 1, cells], ag_ref.at[h, 3, cells], order[1]),
            (agsend_ref.at[h, r, cells], agrecv_ref.at[h, r, cells], order[2]),
        )[stage]
        return along_roll(src, dst, ag_sem, 5 * i + stage + r, dim)

    for stage in range(2):
        for i in range(len(PARTS)):
            gather(i, stage).start()

    for copy in loads[2:5]:
        copy.wait()

    def local_unit(u, _):
        h, r = u // rolls, u % rolls
        view = (r, slice(None), lane(h))
        forward_local(q_ref.at[view], k_ref.at[view], v_ref.at[view], tab_of(h), dec[h], out_ref.at[view], st_ref.at[u])
        return 0

    units = heads * rolls
    def relay(begin, end):
        for i in range(begin, end):
            gather(i, 0).wait()
            gather(i, 2).start()

    lax.fori_loop(0, 3, local_unit, 0)
    relay(0, 3)
    lax.fori_loop(3, 5, local_unit, 0)
    relay(3, len(PARTS))
    lax.fori_loop(5, units, local_unit, 0)
    for copy in tag_copies:
        copy.wait()

    def send_start(i, r):
        h, order, low, size = PARTS[i]
        cells = pl.ds(low, size)
        tags = tags_ref[order[2]]
        agsend_ref[h, r, cells] = choose(tags[r:r + 1, :], [ag_ref[h, k, cells] for k in range(4)], owners_of(order))
        gather(i, 3, r).start()

    def take_start(i, r):
        h, order, low, size = PARTS[i]
        cells = pl.ds(low, size)
        gather(i, 3, r).wait()
        start_ref[h, r, cells] = agrecv_ref[h, r, cells] + choose(wh[r], [ag_ref[h, k, cells] for k in range(4)], owners_of(order))

    for begin, end in ((0, 3), (3, len(PARTS))):
        for i in range(begin, end):
            gather(i, 1).wait()
            gather(i, 2).wait()
            send_start(i, 0)
        for i in range(begin, end):
            send_start(i, 1)
    loads[5].wait()

    def start_units(r, begin, end):
        def unit(h, _):
            view = (r, slice(None), lane(h))
            forward_start(q_ref.at[view], g_ref.at[view], out_ref.at[view], start_ref[h, r], gains_ref[h], sz[r],
                          tab_of(h), dec[h], sq_ref.at[r], cr_ref.at[r], h == 0)
            return 0

        lax.fori_loop(begin, end, unit, 0)

    def pack(total):
        packed = None
        for n in range(count):
            part = jnp.where(line == n, total[:, n * C:(n + 1) * C], 0.0)
            packed = part if packed is None else packed + part
        return packed

    def push(r, i):
        return along_head(msg_ref.at[r], all_ref.at[r, i], ar_sem, len(others) * r + i, others[i])

    def open_sum(r):
        msg_ref[r, 0:8] = pack(row_sums(sq_ref[r]))
        msg_ref[r, 8:16] = pack(row_sums(cr_ref[r]))
        for i in range(len(others)):
            push(r, i).start()

    def close_sum(r):
        for i in range(len(others)):
            push(r, i).wait()
        total = msg_ref[r]
        for i in range(len(others)):
            total = total + all_ref[r, i]
        ss, cross = total[0:8], total[8:16]
        token = line * C + lax.broadcasted_iota(jnp.int32, (8, D), 1)
        scale = jnp.where(token < sz[r], lax.rsqrt(ss / features + EPS), 0.0)
        coef = scale * scale * scale * cross / features
        for n in range(count):
            sb_ref[r, cut(n), :] = column(scale[n:n + 1, :])
            cb_ref[r, cut(n), :] = column(coef[n:n + 1, :])

    def back_units(r, begin, end):
        def unit(h, _):
            view = (r, slice(None), lane(h))
            sg_ref[h, r] = start_back(qs_ref.at[h * rolls + r], g_ref.at[view], out_ref.at[view], sb_ref.at[r], cb_ref.at[r], gains_ref[h], dec[h],
                                      hi_ref.at[view], lo_ref.at[view], back_ref.at[h * rolls + r])
            return 0

        lax.fori_loop(begin, end, unit, 0)

    def scatter(i, stage):
        h, order, low, size = PARTS[i]
        cells = pl.ds(low, size)
        src, dst = (
            (sg_ref.at[h, :, cells], rs1_ref.at[h, :, cells]),
            (acc_ref.at[h, pl.ds(2, 2), cells], rs2_ref.at[h, :, cells]),
            (acc_ref.at[h, pl.ds(1, 1), cells], rs3_ref.at[h, :, cells]),
        )[stage]
        return along_roll(src, dst, rs_sem, 3 * i + stage, order[2 - stage])

    for r in range(rolls):
        for i in range(3):
            take_start(i, r)
        start_units(r, 0, 3)
        for i in range(3, len(PARTS)):
            take_start(i, r)
        start_units(r, 3, heads)
        open_sum(r)

    def ready_unit(u, _):
        h, r = u // rolls, u % rolls
        ready(q_ref.at[r, slice(None), lane(h)], st_ref.at[u], qs_ref.at[u], start_ref[h, r], tab_of(h), dec[h])
        return 0

    lax.fori_loop(0, units, ready_unit, 0)
    for r in range(rolls - 1):
        close_sum(r)
        back_units(r, 0, heads)
    close_sum(rolls - 1)
    for h in range(heads):
        back_units(rolls - 1, h, h + 1)
        for i, part in enumerate(PARTS):
            if part[0] == h:
                scatter(i, 0).start()

    def grad_unit(u, _):
        h, r = u // rolls, u % rolls
        view = (r, slice(None), lane(h))
        backward(q_ref.at[view], k_ref.at[view], v_ref.at[view], hi_ref.at[view], lo_ref.at[view], st_ref.at[u], back_ref.at[u], tab_of(h),
                 dq_ref.at[view], dk_ref.at[view], dv_ref.at[view])
        for n in range(count):
            cells = (r, cut(n), lane(h))
            normed_ref[cells] = (out_ref[cells] * sb_ref[r, cut(n), :] * gains_ref[h]).astype(BF16)
        return 0

    lax.fori_loop(0, 2, grad_unit, 0)
    for i, (h, order, low, size) in enumerate(PARTS):
        cells = pl.ds(low, size)
        tags = tags_ref[order[2]]
        scatter(i, 0).wait()
        for k, owner in enumerate(owners_of(order)):
            total = None
            for r in range(rolls):
                part = jnp.where(wh[r] == owner, sg_ref[h, r, cells], 0.0) + jnp.where(tags[r:r + 1, :] == owner, rs1_ref[h, r, cells], 0.0)
                total = part if total is None else total + part
            acc_ref[h, k, cells] = total
        scatter(i, 1).start()
    lax.fori_loop(2, 6, grad_unit, 0)
    for i, (h, order, low, size) in enumerate(PARTS):
        cells = pl.ds(low, size)
        scatter(i, 1).wait()
        acc_ref[h, 0, cells] += rs2_ref[h, 0, cells]
        acc_ref[h, 1, cells] += rs2_ref[h, 1, cells]
        scatter(i, 2).start()
    lax.fori_loop(6, units, grad_unit, 0)
    for i, (h, order, low, size) in enumerate(PARTS):
        cells = pl.ds(low, size)
        scatter(i, 2).wait()
        owned_ref[h, cells] = acc_ref[h, 0, cells] + rs3_ref[h, 0, cells]


def last_kernel(dec, normed, dq, dk, dv, grad, pk, pv, normed_hbm, dq_hbm, dk_hbm, dv_hbm, gk_hbm, gv_hbm, gk_ref, gv_ref, sem):
    copies = [pltpu.make_async_copy(src, dst, sem.at[i]) for i, (src, dst) in enumerate(
        ((normed, normed_hbm), (dq, dq_hbm), (dk, dk_hbm), (dv, dv_hbm), (gk_ref, gk_hbm.at[0]), (gv_ref, gv_hbm.at[0])))]
    for copy in copies[:4]:
        copy.start()

    def unit(h, _):
        view = (slice(None), pl.ds(pl.multiple_of(h * D, D), D))
        prompt_grads(pk.at[view], pv.at[view], grad[h], tables(dec[h])[3], dec[h], gk_ref.at[view], gv_ref.at[view])
        return 0

    lax.fori_loop(0, grad.shape[0], unit, 0)
    for copy in copies[4:]:
        copy.start()
    for copy in copies:
        copy.wait()


def local(q, k, v, g, pk, pv, which, sizes, decay, gain, features, chips, ring):
    rolls, length, width = q.shape
    heads = width // D
    count = length // C
    units = heads * rolls
    shape = jax.ShapeDtypeStruct
    vmem = pl.BlockSpec(memory_space=pltpu.VMEM)
    tokens = pltpu.VMEM(q.shape, BF16)
    prompt = pltpu.VMEM((length, width), BF16)
    block = lambda *lead: pltpu.VMEM((*lead, D, D), F32)
    dma = lambda *dims: pltpu.SemaphoreType.DMA(dims)
    parts = len(PARTS)
    made = pl.pallas_call(
        functools.partial(main_kernel, features, chips, ring),
        in_specs=[SMEM, SMEM, SMEM, vmem] + [ANY] * 6,
        out_specs=[vmem] * 7,
        out_shape=[tokens] * 4 + [block(heads)] + [prompt] * 2,
        scratch_shapes=[tokens] * 4 + [pltpu.VMEM(q.shape, F32)]
        + [block(units, count)] * 2 + [tokens] * 2 + [pltpu.VMEM((rolls, length, D), F32)] * 4 + [block(heads, 4)]
        + [block(heads, 4), block(heads, 2), block(heads, 2), block(heads, 2)]
        + [block(heads, 2), block(heads, 2), block(heads, 4), block(heads, 2), block(heads, 1)]
        + [pltpu.VMEM((units, count, D, 2 * C), BF16), pltpu.VMEM((heads, 1, D), F32), pltpu.VMEM((8, D), jnp.int32), pltpu.VMEM((3, 8, D), jnp.int32)]
        + [pltpu.VMEM((rolls, 16, D), F32), pltpu.VMEM((rolls, 2 * chips - 1, 16, D), F32)]
        + [dma(6), dma(2, 3), dma(2, 5 * parts), dma(2, 3 * parts), dma(2, rolls * (2 * chips - 1))],
        compiler_params=pltpu.CompilerParams(vmem_limit_bytes=44 * 1024 * 1024, collective_id=0, has_side_effects=True),
    )(decay, which, sizes, gain, q, k, v, g, pk, pv)

    return pl.pallas_call(
        last_kernel,
        in_specs=[SMEM] + [vmem] * 7,
        out_specs=[ANY] * 6,
        out_shape=[shape(q.shape, BF16)] * 4 + [shape(pk.shape, BF16)] * 2,
        scratch_shapes=[prompt] * 2 + [dma(6)],
        compiler_params=pltpu.CompilerParams(vmem_limit_bytes=8 * 1024 * 1024),
    )(decay, *made)


def solution(mesh):
    wide_spec = P("roll", None, "head")
    chips = mesh.shape["head"] // 2
    ring = mesh.shape["roll"] // 2

    def run(q, k, v, g, pk, pv, which, sizes, decay, gain):
        body = functools.partial(local, features=gain.shape[0], chips=chips, ring=ring)
        return jax.shard_map(
            body,
            mesh=mesh,
            in_specs=(wide_spec,) * 6 + (P("roll"), P("roll"), P("head"), P("head")),
            out_specs=(wide_spec,) * 6,
            check_vma=False,
        )(q, k, v, g, pk, pv, which, sizes, decay, gain)

    return run
```

time: 79.9 us -> 55.3 us (0.69); the launches traced: 78.8 us -> 55.2 us
  Pallas kernels: 67.5 us -> 54.4 us
  local copies, waits for them, and re-layouts: 10.6 us -> 0.01 us
    pallas_call x1, Pallas kernels: 63.9 us -> 49.8 us  [local(): pl.pallas_call(functools.partial(main_kernel, features, chips, ring), in_...]
    unnamed x20 -> x2, local copies, waits for them, and re-layouts: 9.32 us -> 0.01 us
    reshape x1 -> x0, local copies, waits for them, and re-layouts: 1.26 us -> none  [local(): gain.reshape(1, width)]
    pallas_call x1, Pallas kernels: 3.63 us -> 4.52 us  [local(): pl.pallas_call(last_kernel, in_specs=[SMEM] + [vmem] * 7, out_specs=[ANY]...]
where the time goes in v3:
time: 55.3 us; the launch traced here: 55.2 us
  Pallas kernels  54.4 us (98%)
  between operations  0.82 us (1%)
    pallas_call x1, Pallas kernels, local(): pl.pallas_call(functools.partial(main_kernel, features, chips, ring), in_...  49.8 us
    pallas_call x1, Pallas kernels, local(): pl.pallas_call(last_kernel, in_specs=[SMEM] + [vmem] * 7, out_specs=[ANY]...  4.52 us

profile of v3, /device:TPU:0, one launch (start us, length us, event | category | flops | bytes accessed | tf_op | source)
XLA Modules:
  0.0 55.2 jit_solution(7377586426199448474)
XLA Ops:
  0.6 0.0 copy-start
  0.6 49.8 %shard_map.145 = (bf16[2,1024,512]{2,1,0:T(8,128)(2,1)S(1)}, bf16[2,1024,512]{2,1,0:T(8,128)(2,1)S(1)}, bf16[2,1024,512]{2,1,0:T(8,128)(2,1)S(1)}, bf16[2,1024,5...) custom-call(s32[4]{0:T(128)} %dec.3, s32[2]{0:T(128)} %wh.1, ...), custom_call_target="tpu_custom_call" | custom-call | tf_op jit(solution)/shard_map/pallas_call | solution.py:499
  50.5 0.0 copy-done
  50.5 4.5 %shard_map.146 = (bf16[2,1024,512]{2,1,0:T(8,128)(2,1)}, bf16[2,1024,512]{2,1,0:T(8,128)(2,1)}, bf16[2,1024,512]{2,1,0:T(8,128)(2,1)}, bf16[2,1024,512]{2,1,0:T(...) custom-call(s32[4]{0:T(128)S(1)} %copy-done, ...), custom_call_target="tpu_custom_call" | custom-call | tf_op jit(solution)/shard_map/pallas_call | solution.py:514
Async XLA Ops:
  0.6 49.9 %copy-start = (s32[4]{0:T(128)S(1)}, s32[4]{0:T(128)}, u32[]{:S(2)}) copy-start(s32[4]{0:T(128)} %dec.3) | copy-start | bytes 52

commit v4 on v3

--- a/solution.py
+++ b/solution.py
@@ -60,38 +60,38 @@
     return low, up, qd, kd
 
 
-def power(exponent, tokens):
-    return jnp.exp(-rate_of(exponent, (1, D)) * float(tokens))
+def powers(exponent, count):
+    return jnp.exp(-rate_of(exponent, (count, D)) * (lax.broadcasted_iota(jnp.int32, (count, D), 0) * C).astype(F32))
 
 
 def cut(n):
     return pl.ds(n * C, C)
 
 
-def state_of_prompt(kp, vp, kd, exponent):
+def state_of_prompt(kp, vp, kd, pw):
     count = kp.shape[0] // C
     total = None
     for n in range(count):
-        vd = vp[cut(n), :].astype(F32) * (kd * power(exponent, C * (count - 1 - n)))
+        vd = vp[cut(n), :].astype(F32) * (kd * pw[count - 1 - n:count - n])
         kt = kp[cut(n), :].T
         part = nn(lanes(kt, kt), tall(vd))
         total = part if total is None else total + part
     return total
 
 
-def prompt_grads(kp, vp, grad, kd, exponent, gk_ref, gv_ref):
+def prompt_grads(kp, vp, grad, kd, pw, gk_ref, gv_ref):
     count = kp.shape[0] // C
     flat, high = wide(grad), tall(grad)
     for n in range(count):
-        decay = kd * power(exponent, C * (count - 1 - n))
+        decay = kd * pw[count - 1 - n:count - n]
         k, v = kp[cut(n), :], vp[cut(n), :]
         gk_ref[cut(n), :] = (nt(lanes(v, v), flat) * decay).astype(BF16)
         gv_ref[cut(n), :] = (nn(lanes(k, k), high) * decay).astype(BF16)
 
 
-def forward_local(q_ref, k_ref, v_ref, tab, exponent, out_ref, state_ref):
+def forward_local(q_ref, k_ref, v_ref, tab, pw, out_ref, state_ref):
     low, up, qd, kd = tab
-    step = power(exponent, C)
+    step = pw[1:2]
     zero = jnp.zeros((D, C), BF16)
     count = q_ref.shape[0] // C
     state_ref[0] = jnp.zeros((D, D), F32)
@@ -112,13 +112,13 @@
         out_ref[cut(n), :] = out
 
 
-def forward_start(q_ref, g_ref, attn_ref, start, gain, size, tab, exponent, sq_ref, cr_ref, first):
+def forward_start(q_ref, g_ref, attn_ref, start, gain, size, tab, pw, sq_ref, cr_ref, first):
     low, up, qd, kd = tab
     high = tall(start)
     for n in range(q_ref.shape[0] // C):
         q = q_ref[cut(n), :]
         token = lax.broadcasted_iota(jnp.int32, (C, D), 0) + n * C
-        attn = attn_ref[cut(n), :] + nn(lanes(q, q), high) * (qd * power(exponent, C * n))
+        attn = attn_ref[cut(n), :] + nn(lanes(q, q), high) * (qd * pw[n:n + 1])
         attn = jnp.where(token < size, attn, 0.0)
         attn_ref[cut(n), :] = attn
         dyg = g_ref[cut(n), :].astype(F32) * gain
@@ -127,10 +127,10 @@
         cr_ref[cut(n), :] = jnp.where(first, 0.0, cr_ref[cut(n), :]) + cross
 
 
-def ready(q_ref, state_ref, qs_ref, start, tab, exponent):
+def ready(q_ref, state_ref, qs_ref, start, tab, pw):
     low, up, qd, kd = tab
     for n in range(q_ref.shape[0] // C):
-        state_ref[n] = state_ref[n] + start * power(exponent, C * n)
+        state_ref[n] = state_ref[n] + start * pw[n:n + 1]
         hi, lo = split(q_ref[cut(n), :].astype(F32) * qd)
         qs_ref[n] = lanes(hi.T, lo.T)
 
@@ -146,8 +146,8 @@
     return nn(wide(spread), jnp.ones((2 * C, D), BF16))
 
 
-def start_back(qs_ref, g_ref, attn_ref, s_ref, c_ref, gain, exponent, hi_ref, lo_ref, grad_ref):
-    step = power(exponent, C)
+def start_back(qs_ref, g_ref, attn_ref, s_ref, c_ref, gain, pw, hi_ref, lo_ref, grad_ref):
+    step = pw[1:2]
     total = None
     count = qs_ref.shape[0]
     for n in reversed(range(count)):
@@ -192,7 +192,10 @@
 SMEM = pl.BlockSpec(memory_space=pltpu.SMEM)
 ANY = pl.BlockSpec(memory_space=pl.ANY)
 TURNS = ((0, 1, 2), (1, 2, 0), (2, 0, 1))
-PARTS = tuple((h, TURNS[h], 0, D) for h in range(3)) + ((3, TURNS[0], 0, 48), (3, TURNS[1], 48, 40), (3, TURNS[2], 88, 40))
+CUTS = ((0, 48), (48, 40), (88, 40))
+PARTS = tuple((h, TURNS[h], 0, D) for h in range(3)) + tuple((3, turn, *piece) for turn, piece in zip(TURNS, CUTS))
+FINE = PARTS
+
 
 def flip(place, dim, ring):
     if dim == 0:
@@ -212,12 +215,12 @@
 
 def main_kernel(
     features, chips, ring,
-    dec, wh, sz, gain_ref, q_hbm, k_hbm, v_hbm, g_hbm, pk_hbm, pv_hbm,
-    normed_ref, dq_ref, dk_ref, dv_ref, owned_ref, pk_ref, pv_ref,
-    q_ref, k_ref, v_ref, g_ref, out_ref, st_ref, back_ref, hi_ref, lo_ref, sq_ref, cr_ref, sb_ref, cb_ref, tab_ref,
+    dec_hbm, wh_hbm, sz_hbm, gain_hbm, q_hbm, k_hbm, v_hbm, g_hbm, pk_hbm, pv_hbm,
+    normed_ref, dq_ref, dk_ref, dv_ref, owned_ref, pk_ref, pv_ref, q_ref, k_ref, v_ref, hi_ref, lo_ref, st_ref, back_ref, tab_ref, pw_ref,
+    g_ref, out_ref, sq_ref, cr_ref, sb_ref, cb_ref,
     ag_ref, agsend_ref, agrecv_ref, start_ref, sg_ref, rs1_ref, acc_ref, rs2_ref, rs3_ref,
-    qs_ref, gains_ref, tag_ref, tags_ref, msg_ref, all_ref,
-    in_sem, tag_sem, ag_sem, rs_sem, ar_sem,
+    dec, wh, sz, gain_ref, qs_ref, gains_ref, tag_ref, tags_ref, msg_ref, all_ref,
+    small_sem, in_sem, tag_sem, ag_sem, rs_sem, ar_sem,
 ):
     rolls, length, width = q_ref.shape
     heads = width // D
@@ -230,9 +233,14 @@
 
     loads = []
     for i, (src, dst) in enumerate(((pk_hbm.at[0], pk_ref), (pv_hbm.at[0], pv_ref), (k_hbm, k_ref), (v_hbm, v_ref), (q_hbm, q_ref), (g_hbm, g_ref))):
-        copy = pltpu.make_async_copy(src, dst, in_sem.at[i])
+        loads.append(pltpu.make_async_copy(src, dst, in_sem.at[i]))
+    for copy in loads[:2]:
         copy.start()
-        loads.append(copy)
+
+    smalls = [pltpu.make_async_copy(src, dst, small_sem.at[i]) for i, (src, dst) in enumerate(
+        ((dec_hbm, dec), (wh_hbm, wh), (sz_hbm, sz), (gain_hbm, gain_ref)))]
+    for copy in smalls:
+        copy.start()
 
     barrier = pltpu.get_barrier_semaphore()
     for place in near:
@@ -250,6 +258,8 @@
             src_ref=src, dst_ref=dst, send_sem=sems.at[0, slot], recv_sem=sems.at[1, slot],
             device_id={"roll": me, "head": place}, device_id_type=MESH)
 
+    for copy in smalls:
+        copy.wait()
     line = lax.broadcasted_iota(jnp.int32, (8, D), 0)
     tag_ref[...] = jnp.where(line == 0, wh[0], wh[1])
 
@@ -262,6 +272,7 @@
         tab_ref[h, 1] = up
         tab_ref[h, 2] = qd
         tab_ref[h, 3] = kd
+        pw_ref[h] = powers(dec[h], max(count, 2))
         return 0
 
     lax.fori_loop(0, heads, fill, 0)
@@ -272,10 +283,12 @@
     def lane(h):
         return pl.ds(pl.multiple_of(h * D, D), D)
 
-    loads[0].wait()
-    loads[1].wait()
+    for copy in loads[:2]:
+        copy.wait()
+    for copy in loads[2:]:
+        copy.start()
     for h in range(heads):
-        ag_ref[h, 0] = state_of_prompt(pk_ref.at[:, lane(h)], pv_ref.at[:, lane(h)], tab_ref[h, 3], dec[h])
+        ag_ref[h, 0] = state_of_prompt(pk_ref.at[:, lane(h)], pv_ref.at[:, lane(h)], tab_ref[h, 3], pw_ref[h])
     pl.semaphore_wait(barrier, 3 + len(others))
 
     tag_copies = [along_roll(tag_ref, tags_ref.at[dim], tag_sem, dim, dim) for dim in range(3)]
@@ -288,7 +301,7 @@
         return [me, one, flip(me, second, ring), flip(one, second, ring)]
 
     def gather(i, stage, r=0):
-        h, order, low, size = PARTS[i]
+        h, order, low, size = FINE[i]
         cells = pl.ds(low, size)
         src, dst, dim = (
             (ag_ref.at[h, 0, cells], ag_ref.at[h, 1, cells], order[0]),
@@ -299,7 +312,7 @@
         return along_roll(src, dst, ag_sem, 5 * i + stage + r, dim)
 
     for stage in range(2):
-        for i in range(len(PARTS)):
+        for i in range(len(FINE)):
             gather(i, stage).start()
 
     for copy in loads[2:5]:
@@ -308,50 +321,52 @@
     def local_unit(u, _):
         h, r = u // rolls, u % rolls
         view = (r, slice(None), lane(h))
-        forward_local(q_ref.at[view], k_ref.at[view], v_ref.at[view], tab_of(h), dec[h], out_ref.at[view], st_ref.at[u])
+        forward_local(q_ref.at[view], k_ref.at[view], v_ref.at[view], tab_of(h), pw_ref[h], out_ref.at[view], st_ref.at[u])
         return 0
 
     units = heads * rolls
+    def parts_of(begin, end):
+        return [i for i, part in enumerate(FINE) if begin <= part[0] < end]
+
     def relay(begin, end):
-        for i in range(begin, end):
+        for i in parts_of(begin, end):
             gather(i, 0).wait()
             gather(i, 2).start()
 
     lax.fori_loop(0, 3, local_unit, 0)
-    relay(0, 3)
+    relay(0, 2)
     lax.fori_loop(3, 5, local_unit, 0)
-    relay(3, len(PARTS))
+    relay(2, heads)
     lax.fori_loop(5, units, local_unit, 0)
     for copy in tag_copies:
         copy.wait()
 
     def send_start(i, r):
-        h, order, low, size = PARTS[i]
+        h, order, low, size = FINE[i]
         cells = pl.ds(low, size)
         tags = tags_ref[order[2]]
         agsend_ref[h, r, cells] = choose(tags[r:r + 1, :], [ag_ref[h, k, cells] for k in range(4)], owners_of(order))
         gather(i, 3, r).start()
 
     def take_start(i, r):
-        h, order, low, size = PARTS[i]
+        h, order, low, size = FINE[i]
         cells = pl.ds(low, size)
         gather(i, 3, r).wait()
         start_ref[h, r, cells] = agrecv_ref[h, r, cells] + choose(wh[r], [ag_ref[h, k, cells] for k in range(4)], owners_of(order))
 
-    for begin, end in ((0, 3), (3, len(PARTS))):
-        for i in range(begin, end):
-            gather(i, 1).wait()
-            gather(i, 2).wait()
-            send_start(i, 0)
-        for i in range(begin, end):
-            send_start(i, 1)
+    for i in range(len(FINE)):
+        gather(i, 1).wait()
+        gather(i, 2).wait()
+        send_start(i, 0)
+    for i in range(len(FINE)):
+        send_start(i, 1)
     loads[5].wait()
 
     def start_units(r, begin, end):
         def unit(h, _):
             view = (r, slice(None), lane(h))
             forward_start(q_ref.at[view], g_ref.at[view], out_ref.at[view], start_ref[h, r], gains_ref[h], sz[r],
-                          tab_of(h), dec[h], sq_ref.at[r], cr_ref.at[r], h == 0)
+                          tab_of(h), pw_ref[h], sq_ref.at[r], cr_ref.at[r], h == 0)
             return 0
 
         lax.fori_loop(begin, end, unit, 0)
@@ -389,7 +404,7 @@
     def back_units(r, begin, end):
         def unit(h, _):
             view = (r, slice(None), lane(h))
-            sg_ref[h, r] = start_back(qs_ref.at[h * rolls + r], g_ref.at[view], out_ref.at[view], sb_ref.at[r], cb_ref.at[r], gains_ref[h], dec[h],
+            sg_ref[h, r] = start_back(qs_ref.at[h * rolls + r], g_ref.at[view], out_ref.at[view], sb_ref.at[r], cb_ref.at[r], gains_ref[h], pw_ref[h],
                                       hi_ref.at[view], lo_ref.at[view], back_ref.at[h * rolls + r])
             return 0
 
@@ -406,17 +421,15 @@
         return along_roll(src, dst, rs_sem, 3 * i + stage, order[2 - stage])
 
     for r in range(rolls):
-        for i in range(3):
-            take_start(i, r)
-        start_units(r, 0, 3)
-        for i in range(3, len(PARTS)):
-            take_start(i, r)
-        start_units(r, 3, heads)
+        for h in range(heads):
+            for i in parts_of(h, h + 1):
+                take_start(i, r)
+            start_units(r, h, h + 1)
         open_sum(r)
 
     def ready_unit(u, _):
         h, r = u // rolls, u % rolls
-        ready(q_ref.at[r, slice(None), lane(h)], st_ref.at[u], qs_ref.at[u], start_ref[h, r], tab_of(h), dec[h])
+        ready(q_ref.at[r, slice(None), lane(h)], st_ref.at[u], qs_ref.at[u], start_ref[h, r], tab_of(h), pw_ref[h])
         return 0
 
     lax.fori_loop(0, units, ready_unit, 0)
@@ -430,14 +443,17 @@
             if part[0] == h:
                 scatter(i, 0).start()
 
+    def norm_unit(h, r):
+        for n in range(count):
+            cells = (r, cut(n), lane(h))
+            normed_ref[cells] = (out_ref[cells] * sb_ref[r, cut(n), :] * gains_ref[h]).astype(BF16)
+
     def grad_unit(u, _):
         h, r = u // rolls, u % rolls
         view = (r, slice(None), lane(h))
         backward(q_ref.at[view], k_ref.at[view], v_ref.at[view], hi_ref.at[view], lo_ref.at[view], st_ref.at[u], back_ref.at[u], tab_of(h),
                  dq_ref.at[view], dk_ref.at[view], dv_ref.at[view])
-        for n in range(count):
-            cells = (r, cut(n), lane(h))
-            normed_ref[cells] = (out_ref[cells] * sb_ref[r, cut(n), :] * gains_ref[h]).astype(BF16)
+        norm_unit(h, r)
         return 0
 
     lax.fori_loop(0, 2, grad_unit, 0)
@@ -452,34 +468,54 @@
                 total = part if total is None else total + part
             acc_ref[h, k, cells] = total
         scatter(i, 1).start()
-    lax.fori_loop(2, 6, grad_unit, 0)
+    lax.fori_loop(2, 5, grad_unit, 0)
     for i, (h, order, low, size) in enumerate(PARTS):
         cells = pl.ds(low, size)
         scatter(i, 1).wait()
         acc_ref[h, 0, cells] += rs2_ref[h, 0, cells]
         acc_ref[h, 1, cells] += rs2_ref[h, 1, cells]
         scatter(i, 2).start()
-    lax.fori_loop(6, units, grad_unit, 0)
+    lax.fori_loop(5, units - 1, grad_unit, 0)
+    norm_unit(heads - 1, rolls - 1)
     for i, (h, order, low, size) in enumerate(PARTS):
         cells = pl.ds(low, size)
         scatter(i, 2).wait()
         owned_ref[h, cells] = acc_ref[h, 0, cells] + rs3_ref[h, 0, cells]
 
 
-def last_kernel(dec, normed, dq, dk, dv, grad, pk, pv, normed_hbm, dq_hbm, dk_hbm, dv_hbm, gk_hbm, gv_hbm, gk_ref, gv_ref, sem):
-    copies = [pltpu.make_async_copy(src, dst, sem.at[i]) for i, (src, dst) in enumerate(
-        ((normed, normed_hbm), (dq, dq_hbm), (dk, dk_hbm), (dv, dv_hbm), (gk_ref, gk_hbm.at[0]), (gv_ref, gv_hbm.at[0])))]
-    for copy in copies[:4]:
+def last_kernel(
+    normed, dq, dk, dv, grad, pk, pv, q, k, v, hi, lo, st, back, tab, pw,
+    normed_hbm, dq_hbm, dk_hbm, dv_hbm, gk_hbm, gv_hbm, dq_ref, dk_ref, dv_ref, gk_ref, gv_ref, sem,
+):
+    rolls, length, width = q.shape
+    heads = width // D
+    h, r = heads - 1, rolls - 1
+    copies = []
+
+    def begin(src, dst):
+        copy = pltpu.make_async_copy(src, dst, sem.at[len(copies)])
         copy.start()
+        copies.append(copy)
+
+    begin(normed, normed_hbm)
+    for src, dst in ((dq, dq_hbm), (dk, dk_hbm), (dv, dv_hbm)):
+        begin(src.at[pl.ds(0, r)], dst.at[pl.ds(0, r)])
+        begin(src.at[r, :, pl.ds(0, h * D)], dst.at[r, :, pl.ds(0, h * D)])
 
     def unit(h, _):
         view = (slice(None), pl.ds(pl.multiple_of(h * D, D), D))
-        prompt_grads(pk.at[view], pv.at[view], grad[h], tables(dec[h])[3], dec[h], gk_ref.at[view], gv_ref.at[view])
+        prompt_grads(pk.at[view], pv.at[view], grad[h], tab[h, 3], pw[h], gk_ref.at[view], gv_ref.at[view])
         return 0
 
-    lax.fori_loop(0, grad.shape[0], unit, 0)
-    for copy in copies[4:]:
-        copy.start()
+    lax.fori_loop(0, heads, unit, 0)
+    begin(gk_ref, gk_hbm.at[0])
+    begin(gv_ref, gv_hbm.at[0])
+    view = (r, slice(None), pl.ds(h * D, D))
+    u = h * rolls + r
+    backward(q.at[view], k.at[view], v.at[view], hi.at[view], lo.at[view], st.at[u], back.at[u], (tab[h, 0], tab[h, 1], tab[h, 2], tab[h, 3]),
+             dq_ref, dk_ref, dv_ref)
+    for src, dst in ((dq_ref, dq_hbm), (dk_ref, dk_hbm), (dv_ref, dv_hbm)):
+        begin(src, dst.at[view])
     for copy in copies:
         copy.wait()
 
@@ -498,27 +534,27 @@
     parts = len(PARTS)
     made = pl.pallas_call(
         functools.partial(main_kernel, features, chips, ring),
-        in_specs=[SMEM, SMEM, SMEM, vmem] + [ANY] * 6,
-        out_specs=[vmem] * 7,
-        out_shape=[tokens] * 4 + [block(heads)] + [prompt] * 2,
-        scratch_shapes=[tokens] * 4 + [pltpu.VMEM(q.shape, F32)]
-        + [block(units, count)] * 2 + [tokens] * 2 + [pltpu.VMEM((rolls, length, D), F32)] * 4 + [block(heads, 4)]
+        in_specs=[ANY] * 10,
+        out_specs=[vmem] * 16,
+        out_shape=[tokens] * 4 + [block(heads)] + [prompt] * 2 + [tokens] * 5 + [block(units, count)] * 2 + [block(heads, 4), pltpu.VMEM((heads, max(count, 2), D), F32)],
+        scratch_shapes=[tokens, pltpu.VMEM(q.shape, F32)] + [pltpu.VMEM((rolls, length, D), F32)] * 4
         + [block(heads, 4), block(heads, 2), block(heads, 2), block(heads, 2)]
         + [block(heads, 2), block(heads, 2), block(heads, 4), block(heads, 2), block(heads, 1)]
+        + [pltpu.SMEM(decay.shape, jnp.int32), pltpu.SMEM(which.shape, jnp.int32), pltpu.SMEM(sizes.shape, jnp.int32), pltpu.VMEM(gain.shape, BF16)]
         + [pltpu.VMEM((units, count, D, 2 * C), BF16), pltpu.VMEM((heads, 1, D), F32), pltpu.VMEM((8, D), jnp.int32), pltpu.VMEM((3, 8, D), jnp.int32)]
         + [pltpu.VMEM((rolls, 16, D), F32), pltpu.VMEM((rolls, 2 * chips - 1, 16, D), F32)]
-        + [dma(6), dma(2, 3), dma(2, 5 * parts), dma(2, 3 * parts), dma(2, rolls * (2 * chips - 1))],
-        compiler_params=pltpu.CompilerParams(vmem_limit_bytes=44 * 1024 * 1024, collective_id=0, has_side_effects=True),
+        + [dma(4), dma(6), dma(2, 3), dma(2, 5 * len(FINE)), dma(2, 3 * parts), dma(2, rolls * (2 * chips - 1))],
+        compiler_params=pltpu.CompilerParams(vmem_limit_bytes=26 * 1024 * 1024, collective_id=0, has_side_effects=True),
     )(decay, which, sizes, gain, q, k, v, g, pk, pv)
 
     return pl.pallas_call(
         last_kernel,
-        in_specs=[SMEM] + [vmem] * 7,
+        in_specs=[vmem] * 16,
         out_specs=[ANY] * 6,
         out_shape=[shape(q.shape, BF16)] * 4 + [shape(pk.shape, BF16)] * 2,
-        scratch_shapes=[prompt] * 2 + [dma(6)],
+        scratch_shapes=[pltpu.VMEM((length, D), BF16)] * 3 + [prompt] * 2 + [dma(12)],
         compiler_params=pltpu.CompilerParams(vmem_limit_bytes=8 * 1024 * 1024),
-    )(decay, *made)
+    )(*made)
 
 
 def solution(mesh):

time: 55.3 us -> 53.4 us (0.966)
  Pallas kernels: 54.4 us -> 52.5 us
    pallas_call x1, Pallas kernels: 49.8 us -> 47.6 us  [local(): pl.pallas_call(functools.partial(main_kernel, features, chips, ring), in_...]
where the time goes in v4:
time: 53.4 us; the launch traced here: 53.3 us
  Pallas kernels  52.5 us (98%)
  between operations  0.8 us (1%)
    pallas_call x1, Pallas kernels, local(): pl.pallas_call(functools.partial(main_kernel, features, chips, ring), in_...  47.6 us
    pallas_call x1, Pallas kernels, local(): pl.pallas_call(last_kernel, in_specs=[vmem] * 16, out_specs=[ANY] * 6, ou...  4.88 us

profile of v4, /device:TPU:0, one launch (start us, length us, event | category | flops | bytes accessed | tf_op | source)
XLA Modules:
  0.0 53.3 jit_solution(9485297084594432042)
XLA Ops:
  0.6 47.6 %shard_map.145 = (bf16[2,1024,512]{2,1,0:T(8,128)(2,1)S(1)}, bf16[2,1024,512]{2,1,0:T(8,128)(2,1)S(1)}, bf16[2,1024,512]{2,1,0:T(8,128)(2,1)S(1)}, bf16[2,1024,5...) custom-call(s32[4]{0:T(128)} %dec_hbm.1, ...), custom_call_target="tpu_custom_call" | custom-call | tf_op jit(solution)/shard_map/pallas_call | solution.py:535
  48.3 4.9 %shard_map.146 = (bf16[2,1024,512]{2,1,0:T(8,128)(2,1)}, bf16[2,1024,512]{2,1,0:T(8,128)(2,1)}, bf16[2,1024,512]{2,1,0:T(8,128)(2,1)}, bf16[2,1024,512]{2,1,0:T(...) custom-call(bf16[2,1024,512]{2,1,0:T(8,128)(2,1)S(1)} %get-tuple-element.22.normed, ...), custom_call_target="tpu_custom_call" | custom-call | tf_op jit(solution)/shard_map/pallas_call | solution.py:550

commit v5 on v4

--- a/solution.py
+++ b/solution.py
@@ -287,8 +287,10 @@
         copy.wait()
     for copy in loads[2:]:
         copy.start()
-    for h in range(heads):
+    def make_state(h):
         ag_ref[h, 0] = state_of_prompt(pk_ref.at[:, lane(h)], pv_ref.at[:, lane(h)], tab_ref[h, 3], pw_ref[h])
+
+    make_state(0)
     pl.semaphore_wait(barrier, 3 + len(others))
 
     tag_copies = [along_roll(tag_ref, tags_ref.at[dim], tag_sem, dim, dim) for dim in range(3)]
@@ -311,9 +313,14 @@
         )[stage]
         return along_roll(src, dst, ag_sem, 5 * i + stage + r, dim)
 
-    for stage in range(2):
-        for i in range(len(FINE)):
-            gather(i, stage).start()
+    for h in range(heads):
+        if h:
+            make_state(h)
+        for i, part in enumerate(FINE):
+            if part[0] == h:
+                gather(i, 0).start()
+    for i in range(len(FINE)):
+        gather(i, 1).start()
 
     for copy in loads[2:5]:
         copy.wait()
@@ -369,7 +376,7 @@
                           tab_of(h), pw_ref[h], sq_ref.at[r], cr_ref.at[r], h == 0)
             return 0
 
-        lax.fori_loop(begin, end, unit, 0)
+        lax.fori_loop(begin, end, unit, 0, unroll=end - begin)
 
     def pack(total):
         packed = None
@@ -408,23 +415,23 @@
                                       hi_ref.at[view], lo_ref.at[view], back_ref.at[h * rolls + r])
             return 0
 
-        lax.fori_loop(begin, end, unit, 0)
-
-    def scatter(i, stage):
+        lax.fori_loop(begin, end, unit, 0, unroll=end - begin)
+
+    def scatter(i, stage, r=0):
         h, order, low, size = PARTS[i]
         cells = pl.ds(low, size)
         src, dst = (
-            (sg_ref.at[h, :, cells], rs1_ref.at[h, :, cells]),
+            (sg_ref.at[h, r, cells], rs1_ref.at[h, r, cells]),
             (acc_ref.at[h, pl.ds(2, 2), cells], rs2_ref.at[h, :, cells]),
             (acc_ref.at[h, pl.ds(1, 1), cells], rs3_ref.at[h, :, cells]),
         )[stage]
-        return along_roll(src, dst, rs_sem, 3 * i + stage, order[2 - stage])
+        return along_roll(src, dst, rs_sem, 4 * i + (stage + 1 if stage else r), order[2 - stage])
 
     for r in range(rolls):
-        for h in range(heads):
-            for i in parts_of(h, h + 1):
+        for begin, end in ((0, 3), (3, heads)):
+            for i in parts_of(begin, end):
                 take_start(i, r)
-            start_units(r, h, h + 1)
+            start_units(r, begin, end)
         open_sum(r)
 
     def ready_unit(u, _):
@@ -436,12 +443,14 @@
     for r in range(rolls - 1):
         close_sum(r)
         back_units(r, 0, heads)
+        for i in range(len(PARTS)):
+            scatter(i, 0, r).start()
     close_sum(rolls - 1)
-    for h in range(heads):
-        back_units(rolls - 1, h, h + 1)
+    for begin, end in ((0, 2), (2, heads)):
+        back_units(rolls - 1, begin, end)
         for i, part in enumerate(PARTS):
-            if part[0] == h:
-                scatter(i, 0).start()
+            if begin <= part[0] < end:
+                scatter(i, 0, rolls - 1).start()
 
     def norm_unit(h, r):
         for n in range(count):
@@ -456,11 +465,12 @@
         norm_unit(h, r)
         return 0
 
-    lax.fori_loop(0, 2, grad_unit, 0)
+    lax.fori_loop(0, 2, grad_unit, 0, unroll=2)
     for i, (h, order, low, size) in enumerate(PARTS):
         cells = pl.ds(low, size)
         tags = tags_ref[order[2]]
-        scatter(i, 0).wait()
+        for r in range(rolls):
+            scatter(i, 0, r).wait()
         for k, owner in enumerate(owners_of(order)):
             total = None
             for r in range(rolls):
@@ -468,14 +478,14 @@
                 total = part if total is None else total + part
             acc_ref[h, k, cells] = total
         scatter(i, 1).start()
-    lax.fori_loop(2, 5, grad_unit, 0)
+    lax.fori_loop(2, 5, grad_unit, 0, unroll=3)
     for i, (h, order, low, size) in enumerate(PARTS):
         cells = pl.ds(low, size)
         scatter(i, 1).wait()
         acc_ref[h, 0, cells] += rs2_ref[h, 0, cells]
         acc_ref[h, 1, cells] += rs2_ref[h, 1, cells]
         scatter(i, 2).start()
-    lax.fori_loop(5, units - 1, grad_unit, 0)
+    lax.fori_loop(5, units - 1, grad_unit, 0, unroll=2)
     norm_unit(heads - 1, rolls - 1)
     for i, (h, order, low, size) in enumerate(PARTS):
         cells = pl.ds(low, size)
@@ -507,7 +517,7 @@
         prompt_grads(pk.at[view], pv.at[view], grad[h], tab[h, 3], pw[h], gk_ref.at[view], gv_ref.at[view])
         return 0
 
-    lax.fori_loop(0, heads, unit, 0)
+    lax.fori_loop(0, heads, unit, 0, unroll=heads)
     begin(gk_ref, gk_hbm.at[0])
     begin(gv_ref, gv_hbm.at[0])
     view = (r, slice(None), pl.ds(h * D, D))
@@ -543,7 +553,7 @@
         + [pltpu.SMEM(decay.shape, jnp.int32), pltpu.SMEM(which.shape, jnp.int32), pltpu.SMEM(sizes.shape, jnp.int32), pltpu.VMEM(gain.shape, BF16)]
         + [pltpu.VMEM((units, count, D, 2 * C), BF16), pltpu.VMEM((heads, 1, D), F32), pltpu.VMEM((8, D), jnp.int32), pltpu.VMEM((3, 8, D), jnp.int32)]
         + [pltpu.VMEM((rolls, 16, D), F32), pltpu.VMEM((rolls, 2 * chips - 1, 16, D), F32)]
-        + [dma(4), dma(6), dma(2, 3), dma(2, 5 * len(FINE)), dma(2, 3 * parts), dma(2, rolls * (2 * chips - 1))],
+        + [dma(4), dma(6), dma(2, 3), dma(2, 5 * len(FINE)), dma(2, 4 * parts), dma(2, rolls * (2 * chips - 1))],
         compiler_params=pltpu.CompilerParams(vmem_limit_bytes=26 * 1024 * 1024, collective_id=0, has_side_effects=True),
     )(decay, which, sizes, gain, q, k, v, g, pk, pv)
 

time: 53.4 us -> 51.7 us (0.968)
  Pallas kernels: 52.5 us -> 50.7 us
    pallas_call x1, Pallas kernels: 47.6 us -> 45.1 us  [local(): pl.pallas_call(functools.partial(main_kernel, features, chips, ring), in_...]
    pallas_call x1, Pallas kernels: 4.88 us -> 5.6 us  [local(): pl.pallas_call(last_kernel, in_specs=[vmem] * 16, out_specs=[ANY] * 6, ou...]
where the time goes in v5:
time: 51.7 us; the launch traced here: 51.5 us
  Pallas kernels  50.7 us (98%)
  between operations  0.82 us (2%)
    pallas_call x1, Pallas kernels, local(): pl.pallas_call(functools.partial(main_kernel, features, chips, ring), in_...  45.1 us
    pallas_call x1, Pallas kernels, local(): pl.pallas_call(last_kernel, in_specs=[vmem] * 16, out_specs=[ANY] * 6, ou...  5.6 us

profile of v5, /device:TPU:0, one launch (start us, length us, event | category | flops | bytes accessed | tf_op | source)
XLA Modules:
  0.0 51.5 jit_solution(5655302459920861509)
XLA Ops:
  0.6 45.1 %shard_map.145 = (bf16[2,1024,512]{2,1,0:T(8,128)(2,1)S(1)}, bf16[2,1024,512]{2,1,0:T(8,128)(2,1)S(1)}, bf16[2,1024,512]{2,1,0:T(8,128)(2,1)S(1)}, bf16[2,1024,5...) custom-call(s32[4]{0:T(128)} %dec_hbm.1, ...), custom_call_target="tpu_custom_call" | custom-call | tf_op jit(solution)/shard_map/pallas_call | solution.py:545
  45.7 5.6 %shard_map.146 = (bf16[2,1024,512]{2,1,0:T(8,128)(2,1)}, bf16[2,1024,512]{2,1,0:T(8,128)(2,1)}, bf16[2,1024,512]{2,1,0:T(8,128)(2,1)}, bf16[2,1024,512]{2,1,0:T(...) custom-call(bf16[2,1024,512]{2,1,0:T(8,128)(2,1)S(1)} %get-tuple-element.22.normed, ...), custom_call_target="tpu_custom_call" | custom-call | tf_op jit(solution)/shard_map/pallas_call | solution.py:560

commit v6 on v5

--- a/solution.py
+++ b/solution.py
@@ -422,10 +422,10 @@
         cells = pl.ds(low, size)
         src, dst = (
             (sg_ref.at[h, r, cells], rs1_ref.at[h, r, cells]),
-            (acc_ref.at[h, pl.ds(2, 2), cells], rs2_ref.at[h, :, cells]),
+            (acc_ref.at[h, 2 + r, cells], rs2_ref.at[h, r, cells]),
             (acc_ref.at[h, pl.ds(1, 1), cells], rs3_ref.at[h, :, cells]),
         )[stage]
-        return along_roll(src, dst, rs_sem, 4 * i + (stage + 1 if stage else r), order[2 - stage])
+        return along_roll(src, dst, rs_sem, 5 * i + 2 * stage + r, order[2 - stage])
 
     for r in range(rolls):
         for begin, end in ((0, 3), (3, heads)):
@@ -471,26 +471,28 @@
         tags = tags_ref[order[2]]
         for r in range(rolls):
             scatter(i, 0, r).wait()
-        for k, owner in enumerate(owners_of(order)):
-            total = None
+        owners = owners_of(order)
+        for k in (3, 2, 1, 0):
+            owner, total = owners[k], None
             for r in range(rolls):
                 part = jnp.where(wh[r] == owner, sg_ref[h, r, cells], 0.0) + jnp.where(tags[r:r + 1, :] == owner, rs1_ref[h, r, cells], 0.0)
                 total = part if total is None else total + part
             acc_ref[h, k, cells] = total
-        scatter(i, 1).start()
+            if k >= 2:
+                scatter(i, 1, k - 2).start()
     lax.fori_loop(2, 5, grad_unit, 0, unroll=3)
     for i, (h, order, low, size) in enumerate(PARTS):
         cells = pl.ds(low, size)
-        scatter(i, 1).wait()
-        acc_ref[h, 0, cells] += rs2_ref[h, 0, cells]
+        scatter(i, 1, 1).wait()
         acc_ref[h, 1, cells] += rs2_ref[h, 1, cells]
         scatter(i, 2).start()
     lax.fori_loop(5, units - 1, grad_unit, 0, unroll=2)
     norm_unit(heads - 1, rolls - 1)
     for i, (h, order, low, size) in enumerate(PARTS):
         cells = pl.ds(low, size)
+        scatter(i, 1, 0).wait()
         scatter(i, 2).wait()
-        owned_ref[h, cells] = acc_ref[h, 0, cells] + rs3_ref[h, 0, cells]
+        owned_ref[h, cells] = acc_ref[h, 0, cells] + rs2_ref[h, 0, cells] + rs3_ref[h, 0, cells]
 
 
 def last_kernel(
@@ -517,13 +519,23 @@
         prompt_grads(pk.at[view], pv.at[view], grad[h], tab[h, 3], pw[h], gk_ref.at[view], gv_ref.at[view])
         return 0
 
-    lax.fori_loop(0, heads, unit, 0, unroll=heads)
+    lax.fori_loop(0, heads, unit, 0)
     begin(gk_ref, gk_hbm.at[0])
     begin(gv_ref, gv_hbm.at[0])
+    u = h * rolls + r
+    half, blocks = length // 2, st.shape[1] // 2
+    table = tab[h, 0], tab[h, 1], tab[h, 2], tab[h, 3]
+
+    def side(i, _):
+        cells = pl.ds(pl.multiple_of(i * half, half), half)
+        view = (r, cells, pl.ds(h * D, D))
+        part = (u, pl.ds(i * blocks, blocks))
+        backward(q.at[view], k.at[view], v.at[view], hi.at[view], lo.at[view], st.at[part], back.at[part], table,
+                 dq_ref.at[cells], dk_ref.at[cells], dv_ref.at[cells])
+        return 0
+
+    lax.fori_loop(0, 2, side, 0)
     view = (r, slice(None), pl.ds(h * D, D))
-    u = h * rolls + r
-    backward(q.at[view], k.at[view], v.at[view], hi.at[view], lo.at[view], st.at[u], back.at[u], (tab[h, 0], tab[h, 1], tab[h, 2], tab[h, 3]),
-             dq_ref, dk_ref, dv_ref)
     for src, dst in ((dq_ref, dq_hbm), (dk_ref, dk_hbm), (dv_ref, dv_hbm)):
         begin(src, dst.at[view])
     for copy in copies:
@@ -553,7 +565,7 @@
         + [pltpu.SMEM(decay.shape, jnp.int32), pltpu.SMEM(which.shape, jnp.int32), pltpu.SMEM(sizes.shape, jnp.int32), pltpu.VMEM(gain.shape, BF16)]
         + [pltpu.VMEM((units, count, D, 2 * C), BF16), pltpu.VMEM((heads, 1, D), F32), pltpu.VMEM((8, D), jnp.int32), pltpu.VMEM((3, 8, D), jnp.int32)]
         + [pltpu.VMEM((rolls, 16, D), F32), pltpu.VMEM((rolls, 2 * chips - 1, 16, D), F32)]
-        + [dma(4), dma(6), dma(2, 3), dma(2, 5 * len(FINE)), dma(2, 4 * parts), dma(2, rolls * (2 * chips - 1))],
+        + [dma(4), dma(6), dma(2, 3), dma(2, 5 * len(FINE)), dma(2, 5 * parts), dma(2, rolls * (2 * chips - 1))],
         compiler_params=pltpu.CompilerParams(vmem_limit_bytes=26 * 1024 * 1024, collective_id=0, has_side_effects=True),
     )(decay, which, sizes, gain, q, k, v, g, pk, pv)
 

time: 51.7 us -> 50.8 us (0.983)
  Pallas kernels: 50.7 us -> 49.9 us
    pallas_call x1, Pallas kernels: 5.6 us -> 4.67 us  [local(): pl.pallas_call(last_kernel, in_specs=[vmem] * 16, out_specs=[ANY] * 6, ou...]
where the time goes in v6:
time: 50.8 us; the launch traced here: 50.7 us
  Pallas kernels  49.9 us (98%)
  between operations  0.82 us (2%)
    pallas_call x1, Pallas kernels, local(): pl.pallas_call(functools.partial(main_kernel, features, chips, ring), in_...  45.2 us
    pallas_call x1, Pallas kernels, local(): pl.pallas_call(last_kernel, in_specs=[vmem] * 16, out_specs=[ANY] * 6, ou...  4.67 us

profile of v6, /device:TPU:0, one launch (start us, length us, event | category | flops | bytes accessed | tf_op | source)
XLA Modules:
  0.0 50.7 jit_solution(320243347474396799)
XLA Ops:
  0.6 45.2 %shard_map.145 = (bf16[2,1024,512]{2,1,0:T(8,128)(2,1)S(1)}, bf16[2,1024,512]{2,1,0:T(8,128)(2,1)S(1)}, bf16[2,1024,512]{2,1,0:T(8,128)(2,1)S(1)}, bf16[2,1024,5...) custom-call(s32[4]{0:T(128)} %dec_hbm.1, ...), custom_call_target="tpu_custom_call" | custom-call | tf_op jit(solution)/shard_map/pallas_call | solution.py:557
  45.8 4.7 %shard_map.146 = (bf16[2,1024,512]{2,1,0:T(8,128)(2,1)}, bf16[2,1024,512]{2,1,0:T(8,128)(2,1)}, bf16[2,1024,512]{2,1,0:T(8,128)(2,1)}, bf16[2,1024,512]{2,1,0:T(...) custom-call(bf16[2,1024,512]{2,1,0:T(8,128)(2,1)S(1)} %get-tuple-element.22.normed, ...), custom_call_target="tpu_custom_call" | custom-call | tf_op jit(solution)/shard_map/pallas_call | solution.py:572
